TPU v7x, 128 devices: a whole 4x4x4 slice. The times are simulated.
128 devices in a mesh: pipe: 8 (over z, core), expert: 16 (over y, x).
Axes of the slice: x: 4, y: 4, z: 4, core: 2. Of those that a mesh axis runs over, the one named last changes fastest.
Arguments:
- a_init: bfloat16 [8, 2048, 3584], P('pipe', 'expert'), may hold values from -6 to 6
- b_init: bfloat16 [8, 2048, 3584], P('pipe', 'expert'), may hold values from -6 to 6
- incoming: bfloat16 [1, 2048, 3584], P(None, 'expert'), may hold values from -6 to 6
- routes: int32 [8, 2, 2, 2048, 1], P('pipe', None, None, 'expert'), may hold values from 0 to 7; in each aligned block of 128 rows (0 to 127, 128 to 255, ..., all dimensions but the last counted through in order) at most 20 rows name the same one
- gain: bfloat16 [8, 2, 3584], P('pipe'), may hold values from 0.5 to 1.5
- router: bfloat16 [8, 2, 3584, 8], P('pipe'), may hold values from -0.09375 to 0.09375
- w_gate: bfloat16 [8, 2, 3584, 8192], P('pipe', None, None, 'expert'), may hold values from -0.09375 to 0.09375
- w_up: bfloat16 [8, 2, 3584, 8192], P('pipe', None, None, 'expert'), may hold values from -0.09375 to 0.09375
- w_down: bfloat16 [8, 2, 8192, 3584], P('pipe', None, 'expert'), may hold values from -0.1875 to 0.1875
Outputs:
- out_a: bfloat16 [2, 8, 2048, 3584], P(None, 'pipe', 'expert')
- out_b: bfloat16 [2, 8, 2048, 3584], P(None, 'pipe', 'expert')
Inputs may be any that keep to these rules, and one draw needn't show every extreme that they name: `routes`: in each aligned block of 128 rows (one device's tokens of one slot and step) no expert is named more than 20 times, a bound that some block reaches.
All inputs are finite; a program needn't handle non-finite values.
Results may differ from a plain program's by a relative error of at most 0.014.
Values may be sent and summed in bfloat16 or wider, within the bound.
A program may use at most 192 MiB of HBM per device.

v0:
```python
import jax
import jax.numpy as jnp
from jax import lax
from jax.sharding import PartitionSpec as P

ROUTE_GAIN = 2.5


def passed_along(value, axis, steps):
    count = lax.axis_size(axis)
    leading, last = (max(0, -steps), min(count, count - steps))
    return lax.ppermute(value, axis, [(source, source + steps) for source in range(leading, last)])


def prepare(tokens_in, route_ids, gain_row, router_mat, expert_count, capacity):
    values = tokens_in.astype(jnp.float32)
    mean_square = jnp.mean(values * values, axis=-1, keepdims=True)
    normed = (values * lax.rsqrt(mean_square + 1e-06) * gain_row.astype(jnp.float32)).astype(
        jnp.bfloat16
    )
    logits = jnp.dot(normed, router_mat, preferred_element_type=jnp.float32)
    chosen = route_ids[:, 0]
    onehot = (chosen[:, None] == jnp.arange(expert_count, dtype=jnp.int32)[None, :]).astype(
        jnp.int32
    )
    weight = ROUTE_GAIN * jax.nn.sigmoid(jnp.sum(logits * onehot.astype(jnp.float32), axis=-1))
    slot_index = jnp.sum((jnp.cumsum(onehot, axis=0) - 1) * onehot, axis=-1)
    position = chosen * capacity + slot_index
    return (normed, weight, position)


def pack_rows(normed, position, expert_count, capacity):
    columns = jnp.arange(expert_count * capacity, dtype=jnp.int32)
    selector = (position[None, :] == columns[:, None]).astype(jnp.bfloat16)
    packed = jnp.dot(selector, normed, preferred_element_type=jnp.float32).astype(jnp.bfloat16)
    return packed.reshape(expert_count, capacity, normed.shape[1])


def apply_expert(rows, gate_mat, up_mat, down_mat):
    flat = rows.reshape(-1, rows.shape[-1])
    gate_val = jnp.dot(flat, gate_mat, preferred_element_type=jnp.float32)
    up_val = jnp.dot(flat, up_mat, preferred_element_type=jnp.float32)
    hidden = (jax.nn.silu(gate_val) * up_val).astype(jnp.bfloat16)
    partial_value = jnp.dot(hidden, down_mat, preferred_element_type=jnp.float32).astype(
        jnp.bfloat16
    )
    return partial_value.reshape(rows.shape)


def unpack_rows(returned, position, expert_count):
    copies = returned.shape[0] // expert_count
    summed = (
        returned.astype(jnp.float32)
        .reshape(expert_count, copies, returned.shape[1], returned.shape[2])
        .sum(axis=1)
    )
    return jnp.take(summed.reshape(-1, returned.shape[2]), position, axis=0)


def body(a_init, b_init, incoming, routes, gain, router, w_gate, w_up, w_down):
    expert_count = router.shape[-1]
    expert_devices = lax.axis_size("expert")
    copies = expert_devices // expert_count
    tok_rows = a_init.shape[1]
    capacity = 5 * tok_rows // (4 * expert_count)
    pipe_rank = lax.axis_index("pipe")
    last_rank = lax.axis_size("pipe") - 1
    step_count = routes.shape[1]

    def weights_of(group):
        return (w_gate[0, group], w_up[0, group], w_down[0, group])

    def layer_pair(forward, backward, step_index):
        states = (forward, backward)
        prepared = [
            prepare(
                states[group],
                routes[0, step_index, group],
                gain[0, group],
                router[0, group],
                expert_count,
                capacity,
            )
            for group in (0, 1)
        ]
        packs = [
            pack_rows(prepared[group][0], prepared[group][2], expert_count, capacity)
            for group in (0, 1)
        ]
        sends = [jnp.repeat(packs[group], copies, axis=0) for group in (0, 1)]
        returned = (
            lax.all_to_all(
                apply_expert(
                    lax.all_to_all(sends[0], "expert", split_axis=0, concat_axis=0, tiled=True),
                    *weights_of(0)
                ),
                "expert",
                split_axis=0,
                concat_axis=0,
                tiled=True,
            ),
            lax.all_to_all(
                apply_expert(
                    lax.all_to_all(sends[1], "expert", split_axis=0, concat_axis=0, tiled=True),
                    *weights_of(1)
                ),
                "expert",
                split_axis=0,
                concat_axis=0,
                tiled=True,
            ),
        )
        expert_outs = [
            unpack_rows(returned[group], prepared[group][2], expert_count) for group in (0, 1)
        ]
        results = []
        for group in (0, 1):
            values = states[group].astype(jnp.float32)
            results.append(
                (values + prepared[group][1][:, None] * expert_outs[group]).astype(jnp.bfloat16)
            )
        return (results[0], results[1])

    forward = a_init[0]
    backward = b_init[0]
    outs_a = []
    outs_b = []
    for step_index in range(step_count):
        out_fwd, out_bwd = layer_pair(forward, backward, step_index)
        outs_a.append(out_fwd)
        outs_b.append(out_bwd)
        if step_index + 1 < step_count:
            moved = passed_along(out_fwd, "pipe", 1)
            forward = jnp.where(pipe_rank == 0, incoming[step_index], moved)
            moved_back = passed_along(out_bwd, "pipe", -1)
            backward = jnp.where(pipe_rank == last_rank, out_fwd, moved_back)
    return (jnp.stack(outs_a)[:, None], jnp.stack(outs_b)[:, None])


def solution(mesh):
    placed = (
        P("pipe", "expert", None),
        P("pipe", "expert", None),
        P(None, "expert", None),
        P("pipe", None, None, "expert", None),
        P("pipe", None, None),
        P("pipe", None, None, None),
        P("pipe", None, None, "expert"),
        P("pipe", None, None, "expert"),
        P("pipe", None, "expert", None),
    )
    return jax.shard_map(
        body,
        mesh=mesh,
        in_specs=placed,
        out_specs=(P(None, "pipe", "expert", None), P(None, "pipe", "expert", None)),
        check_vma=False,
    )
```

profile of v0, /device:TPU:100, one launch (start us, length us, event | category | flops | bytes accessed | tf_op | source)
XLA Modules:
  0.0 385.6 jit_solution(5891294021018272392)
XLA Ops:
  8.6 7.4 %all-to-all-start.4 = ((bf16[16,20,3584]{2,1,0:T(8,128)(2,1)}), bf16[16,20,3584]{2,1,0:T(8,128)(2,1)S(1)}, u32[]{:S(2)}, u32[]{:S(2)}) async-start(bf16[16,20,3584]{2,1,0:T(8,128)(2,1)} %bitcast.169), calls=%async_computation.4 | async-start | bytes 5505024 | tf_op jit(solution)/shard_map/all_to_all | solution.py:104
  22.4 30.0 %all-to-all-done.4 = bf16[16,20,3584]{2,1,0:T(8,128)(2,1)S(1)} async-done(((bf16[16,20,3584]{2,1,0:T(8,128)(2,1)}), bf16[16,20,3584]{2,1,0:T(8,128)(2,1)S(1)}, u32[]{:S(2)}, u32[]{:S(2)}) %all-to-all-start.4) | async-done | bytes 2293792 | tf_op jit(solution)/shard_map/all_to_all | solution.py:104
  56.6 9.0 %all-to-all-start = ((bf16[16,20,3584]{2,1,0:T(8,128)(2,1)}), bf16[16,20,3584]{2,1,0:T(8,128)(2,1)S(1)}, u32[]{:S(2)}, u32[]{:S(2)}) async-start(bf16[16,20,3584]{2,1,0:T(8,128)(2,1)} %bitcast.168), calls=%async_computation | async-start | bytes 5505024 | tf_op jit(solution)/shard_map/all_to_all | solution.py:94
  69.7 4.9 %fusion.8 = f32[320,512]{1,0:T(8,128)} fusion(bf16[320,3584]{1,0:T(8,128)(2,1)} %reshape.251, bf16[1,2,3584,512]{3,2,1,0:T(8,128)(2,1)} %param.17), kind=kOutput, calls=%fused_computation.24 | convolution fusion | flops 1174405120 | bytes 6619136 | tf_op jit(solution)/shard_map/dot_general | solution.py:41
  74.6 8.1 %convolution_convert_fusion.1 = bf16[320,3584]{1,0:T(8,128)(2,1)} fusion(bf16[1,2,512,3584]{3,2,1,0:T(8,128)(2,1)} %param.19, bf16[320,3584]{1,0:T(8,128)(2,1)} %reshape.251, bf16[1,2,3584,512]{3,2,1,0:T(8,128)(2,1)} %param.18, f32[320,512]{1,0:T(8,128)} %fusion.8), kind=kOutput, calls=%fused_computation.9 | convolution fusion | flops 2350940160 | bytes 12582912 | tf_op jit(solution)/shard_map/dot_general | solution.py:44
  86.8 12.8 %all-to-all-done = bf16[16,20,3584]{2,1,0:T(8,128)(2,1)S(1)} async-done(((bf16[16,20,3584]{2,1,0:T(8,128)(2,1)}), bf16[16,20,3584]{2,1,0:T(8,128)(2,1)S(1)}, u32[]{:S(2)}, u32[]{:S(2)}) %all-to-all-start) | async-done | bytes 2293792 | tf_op jit(solution)/shard_map/all_to_all | solution.py:94
  101.2 8.1 %all-to-all-start.5 = ((bf16[16,20,3584]{2,1,0:T(8,128)(2,1)}), bf16[16,20,3584]{2,1,0:T(8,128)(2,1)S(1)}, u32[]{:S(2)}, u32[]{:S(2)}) async-start(bf16[16,20,3584]{2,1,0:T(8,128)(2,1)} %reshape.252), calls=%async_computation.5 | async-start | bytes 5505024 | tf_op jit(solution)/shard_map/all_to_all | solution.py:102
  115.1 4.9 %fusion.18 = f32[320,512]{1,0:T(8,128)} fusion(bf16[320,3584]{1,0:T(8,128)(2,1)} %reshape.237, bf16[1,2,3584,512]{3,2,1,0:T(8,128)(2,1)} %param.17), kind=kOutput, calls=%fused_computation.34 | convolution fusion | flops 1174405120 | bytes 6619136 | tf_op jit(solution)/shard_map/dot_general | solution.py:41
  120.0 8.1 %convolution_convert_fusion.3 = bf16[320,3584]{1,0:T(8,128)(2,1)} fusion(bf16[1,2,512,3584]{3,2,1,0:T(8,128)(2,1)} %param.19, bf16[320,3584]{1,0:T(8,128)(2,1)} %reshape.237, bf16[1,2,3584,512]{3,2,1,0:T(8,128)(2,1)} %param.18, f32[320,512]{1,0:T(8,128)} %fusion.18), kind=kOutput, calls=%fused_computation.11 | convolution fusion | flops 2350940160 | bytes 12582912 | tf_op jit(solution)/shard_map/dot_general | solution.py:44
  132.3 12.0 %all-to-all-done.5 = bf16[16,20,3584]{2,1,0:T(8,128)(2,1)S(1)} async-done(((bf16[16,20,3584]{2,1,0:T(8,128)(2,1)}), bf16[16,20,3584]{2,1,0:T(8,128)(2,1)S(1)}, u32[]{:S(2)}, u32[]{:S(2)}) %all-to-all-start.5) | async-done | bytes 2293792 | tf_op jit(solution)/shard_map/all_to_all | solution.py:102
  144.3 8.6 %all-to-all-start.1 = ((bf16[16,20,3584]{2,1,0:T(8,128)(2,1)}), bf16[16,20,3584]{2,1,0:T(8,128)(2,1)}, u32[]{:S(2)}, u32[]{:S(2)}) async-start(bf16[16,20,3584]{2,1,0:T(8,128)(2,1)} %reshape.238), calls=%async_computation.1 | async-start | bytes 5505024 | tf_op jit(solution)/shard_map/all_to_all | solution.py:92
  165.0 21.3 %all-to-all-done.1 = bf16[16,20,3584]{2,1,0:T(8,128)(2,1)} async-done(((bf16[16,20,3584]{2,1,0:T(8,128)(2,1)}), bf16[16,20,3584]{2,1,0:T(8,128)(2,1)}, u32[]{:S(2)}, u32[]{:S(2)}) %all-to-all-start.1) | async-done | bytes 2293792 | tf_op jit(solution)/shard_map/all_to_all | solution.py:92
  201.5 7.6 %all-to-all-start.6 = ((bf16[16,20,3584]{2,1,0:T(8,128)(2,1)}), bf16[16,20,3584]{2,1,0:T(8,128)(2,1)S(1)}, u32[]{:S(2)}, u32[]{:S(2)}) async-start(bf16[16,20,3584]{2,1,0:T(8,128)(2,1)} %bitcast.166), calls=%async_computation.6 | async-start | bytes 5505024 | tf_op jit(solution)/shard_map/all_to_all | solution.py:104
  211.1 13.1 %collective-permute-done = bf16[128,3584]{1,0:T(8,128)(2,1)} collective-permute-done((bf16[128,3584]{1,0:T(8,128)(2,1)}, bf16[128,3584]{1,0:T(8,128)(2,1)}, u32[]{:S(2)}, u32[]{:S(2)}) %collective-permute-start) | collective-permute-done | bytes 917536 | tf_op jit(solution)/shard_map/ppermute | solution.py:12
  230.8 13.2 %all-to-all-done.6 = bf16[16,20,3584]{2,1,0:T(8,128)(2,1)S(1)} async-done(((bf16[16,20,3584]{2,1,0:T(8,128)(2,1)}), bf16[16,20,3584]{2,1,0:T(8,128)(2,1)S(1)}, u32[]{:S(2)}, u32[]{:S(2)}) %all-to-all-start.6) | async-done | bytes 2293792 | tf_op jit(solution)/shard_map/all_to_all | solution.py:104
  247.1 8.6 %all-to-all-start.2 = ((bf16[16,20,3584]{2,1,0:T(8,128)(2,1)}), bf16[16,20,3584]{2,1,0:T(8,128)(2,1)}, u32[]{:S(2)}, u32[]{:S(2)}) async-start(bf16[16,20,3584]{2,1,0:T(8,128)(2,1)} %bitcast.167), calls=%async_computation.2 | async-start | bytes 5505024 | tf_op jit(solution)/shard_map/all_to_all | solution.py:94
  257.8 5.1 %fusion.6 = f32[320,512]{1,0:T(8,128)} fusion(bf16[320,3584]{1,0:T(8,128)(2,1)} %reshape.258, bf16[1,2,3584,512]{3,2,1,0:T(8,128)(2,1)} %param.17), kind=kOutput, calls=%fused_computation.22 | convolution fusion | flops 1174405120 | bytes 6619136 | tf_op jit(solution)/shard_map/dot_general | solution.py:41
  262.9 7.4 %convolution_convert_fusion = bf16[320,3584]{1,0:T(8,128)(2,1)} fusion(bf16[1,2,512,3584]{3,2,1,0:T(8,128)(2,1)} %param.19, bf16[320,3584]{1,0:T(8,128)(2,1)S(1)} %copy-done.9, bf16[1,2,3584,512]{3,2,1,0:T(8,128)(2,1)} %param.18, f32[320,512]{1,0:T(8,128)} %fusion.6), kind=kOutput, calls=%fused_computation.8 | convolution fusion | flops 2350940160 | bytes 12582912 | tf_op jit(solution)/shard_map/dot_general | solution.py:44
  274.4 14.6 %all-to-all-done.2 = bf16[16,20,3584]{2,1,0:T(8,128)(2,1)} async-done(((bf16[16,20,3584]{2,1,0:T(8,128)(2,1)}), bf16[16,20,3584]{2,1,0:T(8,128)(2,1)}, u32[]{:S(2)}, u32[]{:S(2)}) %all-to-all-start.2) | async-done | bytes 2293792 | tf_op jit(solution)/shard_map/all_to_all | solution.py:94
  289.1 7.6 %all-to-all-start.7 = ((bf16[16,20,3584]{2,1,0:T(8,128)(2,1)}), bf16[16,20,3584]{2,1,0:T(8,128)(2,1)S(1)}, u32[]{:S(2)}, u32[]{:S(2)}) async-start(bf16[16,20,3584]{2,1,0:T(8,128)(2,1)} %reshape.259), calls=%async_computation.7 | async-start | bytes 5505024 | tf_op jit(solution)/shard_map/all_to_all | solution.py:102
  307.4 8.1 %convolution_convert_fusion.2 = bf16[320,3584]{1,0:T(8,128)(2,1)} fusion(bf16[1,2,512,3584]{3,2,1,0:T(8,128)(2,1)} %param.19, bf16[320,3584]{1,0:T(8,128)(2,1)} %reshape.244, bf16[1,2,3584,512]{3,2,1,0:T(8,128)(2,1)} %param.18, f32[320,512]{1,0:T(8,128)} %fusion.16), kind=kOutput, calls=%fused_computation.10 | convolution fusion | flops 2350940160 | bytes 12582912 | tf_op jit(solution)/shard_map/dot_general | solution.py:44
  319.6 12.3 %all-to-all-done.7 = bf16[16,20,3584]{2,1,0:T(8,128)(2,1)S(1)} async-done(((bf16[16,20,3584]{2,1,0:T(8,128)(2,1)}), bf16[16,20,3584]{2,1,0:T(8,128)(2,1)S(1)}, u32[]{:S(2)}, u32[]{:S(2)}) %all-to-all-start.7) | async-done | bytes 2293792 | tf_op jit(solution)/shard_map/all_to_all | solution.py:102
  331.9 9.1 %all-to-all-start.3 = ((bf16[16,20,3584]{2,1,0:T(8,128)(2,1)}), bf16[16,20,3584]{2,1,0:T(8,128)(2,1)}, u32[]{:S(2)}, u32[]{:S(2)}) async-start(bf16[16,20,3584]{2,1,0:T(8,128)(2,1)} %reshape.245), calls=%async_computation.3 | async-start | bytes 5505024 | tf_op jit(solution)/shard_map/all_to_all | solution.py:92
  353.5 20.4 %all-to-all-done.3 = bf16[16,20,3584]{2,1,0:T(8,128)(2,1)} async-done(((bf16[16,20,3584]{2,1,0:T(8,128)(2,1)}), bf16[16,20,3584]{2,1,0:T(8,128)(2,1)}, u32[]{:S(2)}, u32[]{:S(2)}) %all-to-all-start.3) | async-done | bytes 2293792 | tf_op jit(solution)/shard_map/all_to_all | solution.py:92
  (108 shorter events, 122.1 us)
Async XLA Ops:
  0.6 5.3 %copy-start.5 = (bf16[1,128,3584]{2,1,0:T(8,128)(2,1)S(1)}, bf16[1,128,3584]{2,1,0:T(8,128)(2,1)}, u32[]{:S(2)}) copy-start(bf16[1,128,3584]{2,1,0:T(8,128)(2,1)} %param.12) | copy-start | bytes 2752516
  8.6 43.9 %all-to-all-start.4 = ((bf16[16,20,3584]{2,1,0:T(8,128)(2,1)}), bf16[16,20,3584]{2,1,0:T(8,128)(2,1)S(1)}, u32[]{:S(2)}, u32[]{:S(2)}) async-start(bf16[16,20,3584]{2,1,0:T(8,128)(2,1)} %bitcast.169), calls=%async_computation.4 | async-start | bytes 5505024 | tf_op jit(solution)/shard_map/all_to_all | solution.py:104
  52.5 4.1 %copy-start.1 = (bf16[16,20,3584]{2,1,0:T(8,128)(2,1)}, bf16[16,20,3584]{2,1,0:T(8,128)(2,1)S(1)}, u32[]{:S(2)}) copy-start(bf16[16,20,3584]{2,1,0:T(8,128)(2,1)S(1)} %all-to-all-done.4) | copy-start | bytes 6881284
  56.6 43.1 %all-to-all-start = ((bf16[16,20,3584]{2,1,0:T(8,128)(2,1)}), bf16[16,20,3584]{2,1,0:T(8,128)(2,1)S(1)}, u32[]{:S(2)}, u32[]{:S(2)}) async-start(bf16[16,20,3584]{2,1,0:T(8,128)(2,1)} %bitcast.168), calls=%async_computation | async-start | bytes 5505024 | tf_op jit(solution)/shard_map/all_to_all | solution.py:94
  86.8 22.5 %copy-start.10 = (bf16[1,2,3584,8]{2,3,1,0:T(8,128)(2,1)S(1)}, bf16[1,2,3584,8]{2,3,1,0:T(8,128)(2,1)}, u32[]{:S(2)}) copy-start(bf16[1,2,3584,8]{2,3,1,0:T(8,128)(2,1)} %param.16) | copy-start | bytes 344068
  99.7 1.6 copy-start
  101.2 43.0 %all-to-all-start.5 = ((bf16[16,20,3584]{2,1,0:T(8,128)(2,1)}), bf16[16,20,3584]{2,1,0:T(8,128)(2,1)S(1)}, u32[]{:S(2)}, u32[]{:S(2)}) async-start(bf16[16,20,3584]{2,1,0:T(8,128)(2,1)} %reshape.252), calls=%async_computation.5 | async-start | bytes 5505024 | tf_op jit(solution)/shard_map/all_to_all | solution.py:102
  144.3 42.0 %all-to-all-start.1 = ((bf16[16,20,3584]{2,1,0:T(8,128)(2,1)}), bf16[16,20,3584]{2,1,0:T(8,128)(2,1)}, u32[]{:S(2)}, u32[]{:S(2)}) async-start(bf16[16,20,3584]{2,1,0:T(8,128)(2,1)} %reshape.238), calls=%async_computation.1 | async-start | bytes 5505024 | tf_op jit(solution)/shard_map/all_to_all | solution.py:92
  159.3 5.3 %copy-start.2 = (bf16[1,128,3584]{2,1,0:T(8,128)(2,1)S(1)}, bf16[1,128,3584]{2,1,0:T(8,128)(2,1)}, u32[]{:S(2)}) copy-start(bf16[1,128,3584]{2,1,0:T(8,128)(2,1)} %param.11) | copy-start | bytes 2752516
  162.4 32.3 %collective-permute-start.1 = (bf16[128,3584]{1,0:T(8,128)(2,1)}, bf16[128,3584]{1,0:T(8,128)(2,1)}, u32[]{:S(2)}, u32[]{:S(2)}) collective-permute-start(bf16[128,3584]{1,0:T(8,128)(2,1)} %fusion.47), channel_id=1, source_target_pairs={{16,0},{32,16},{48,32},{64,48},{80,64},{96,80},{112,96},{17,1},{33... | collective-permute-start | bytes 2752520 | tf_op jit(solution)/shard_map/ppermute | solution.py:12
  198.0 0.9 copy-start.3
  201.5 42.5 %all-to-all-start.6 = ((bf16[16,20,3584]{2,1,0:T(8,128)(2,1)}), bf16[16,20,3584]{2,1,0:T(8,128)(2,1)S(1)}, u32[]{:S(2)}, u32[]{:S(2)}) async-start(bf16[16,20,3584]{2,1,0:T(8,128)(2,1)} %bitcast.166), calls=%async_computation.6 | async-start | bytes 5505024 | tf_op jit(solution)/shard_map/all_to_all | solution.py:104
  209.1 15.0 %collective-permute-start = (bf16[128,3584]{1,0:T(8,128)(2,1)}, bf16[128,3584]{1,0:T(8,128)(2,1)}, u32[]{:S(2)}, u32[]{:S(2)}) collective-permute-start(bf16[128,3584]{1,0:T(8,128)(2,1)} %get-tuple-element.13), channel_id=1, source_target_pairs={{0,16},{16,32},{32,48},{48,64},{64,80},{80,96},{96,112},{1,17},{17... | collective-permute-start | bytes 2752520 | tf_op jit(solution)/shard_map/ppermute | solution.py:12
  226.0 1.0 copy-start.6
  247.1 42.0 %all-to-all-start.2 = ((bf16[16,20,3584]{2,1,0:T(8,128)(2,1)}), bf16[16,20,3584]{2,1,0:T(8,128)(2,1)}, u32[]{:S(2)}, u32[]{:S(2)}) async-start(bf16[16,20,3584]{2,1,0:T(8,128)(2,1)} %bitcast.167), calls=%async_computation.2 | async-start | bytes 5505024 | tf_op jit(solution)/shard_map/all_to_all | solution.py:94
  257.8 5.1 %copy-start.9 = (bf16[320,3584]{1,0:T(8,128)(2,1)S(1)}, bf16[320,3584]{1,0:T(8,128)(2,1)}, u32[]{:S(2)}) copy-start(bf16[320,3584]{1,0:T(8,128)(2,1)} %reshape.258) | copy-start | bytes 6881284
  289.1 42.9 %all-to-all-start.7 = ((bf16[16,20,3584]{2,1,0:T(8,128)(2,1)}), bf16[16,20,3584]{2,1,0:T(8,128)(2,1)S(1)}, u32[]{:S(2)}, u32[]{:S(2)}) async-start(bf16[16,20,3584]{2,1,0:T(8,128)(2,1)} %reshape.259), calls=%async_computation.7 | async-start | bytes 5505024 | tf_op jit(solution)/shard_map/all_to_all | solution.py:102
  331.9 41.9 %all-to-all-start.3 = ((bf16[16,20,3584]{2,1,0:T(8,128)(2,1)}), bf16[16,20,3584]{2,1,0:T(8,128)(2,1)}, u32[]{:S(2)}, u32[]{:S(2)}) async-start(bf16[16,20,3584]{2,1,0:T(8,128)(2,1)} %reshape.245), calls=%async_computation.3 | async-start | bytes 5505024 | tf_op jit(solution)/shard_map/all_to_all | solution.py:92
  346.6 2.4 copy-start.4
  379.8 2.4 copy-start.7
  382.2 1.9 copy-start.8
where the time goes:
time: 392 us; the launch traced here: 386 us
  waiting for transfers between devices  150 us (38%)
  starting transfers between devices  70.2 us (18%)
  local copies, waits for them, and re-layouts  68.8 us (18%)
  matrix products  62.1 us (16%)
  other arithmetic  33.7 us (9%)
    all_to_all x2, waiting for transfers between devices, layer_pair(): lax.all_to_all(sends[1], 'expert', split_axis=0, concat_axis=0, tiled=True)  43.2 us
    all_to_all x2, waiting for transfers between devices, layer_pair(): lax.all_to_all(apply_expert(lax.all_to_all(sends[0], 'expert', split_axis...  41.6 us
    dot_general x4, matrix products, apply_expert(): jnp.dot(hidden, down_mat, preferred_element_type=jnp.float32)  31.7 us
    all_to_all x2, waiting for transfers between devices, layer_pair(): lax.all_to_all(sends[0], 'expert', split_axis=0, concat_axis=0, tiled=True)  27.5 us
    all_to_all x2, waiting for transfers between devices, layer_pair(): lax.all_to_all(apply_expert(lax.all_to_all(sends[1], 'expert', split_axis...  24.3 us
    dot_general x4, matrix products, apply_expert(): gate_val = jnp.dot(flat, gate_mat, preferred_element_type=jnp.float32)  19.8 us
    all_to_all x2, starting transfers between devices, layer_pair(): lax.all_to_all(apply_expert(lax.all_to_all(sends[0], 'expert', split_axis...  17.7 us
    all_to_all x2, starting transfers between devices, layer_pair(): lax.all_to_all(sends[0], 'expert', split_axis=0, concat_axis=0, tiled=True)  17.7 us
  transfers between devices with their start and end apart: 10, of which 9 were waited for; matrix products, arithmetic and copies ran while one was open for 33% of the time, Pallas kernels for 0%

commit v1 on v0

v1 whole, which is shorter than its diff:
```python
import functools

import jax
import jax.numpy as jnp
from jax import lax
from jax.experimental import pallas as pl
from jax.experimental.pallas import tpu as pltpu
from jax.sharding import PartitionSpec as P

MESH = pl.DeviceIdType.MESH
F32, BF16, I32 = jnp.float32, jnp.bfloat16, jnp.int32
ROUTE_GAIN = 2.5
SIDE = 4
PARTS = 8
HEAD, TAIL, QUARTERS = 16, 4, 4
WINDOW = 3


def iota(shape, axis):
    return lax.broadcasted_iota(I32, shape, axis)


def ones_where(mask):
    return jnp.where(mask, 1.0, 0.0).astype(BF16)


def dot(left, right):
    return jnp.dot(left, right, preferred_element_type=F32)


def relay(
    pipe_count,
    a_in, b_in, later_in, routes, gain, router, gate_in, up_in, down_in,
    a_out, b_out,
    gate, up, down, own_x, near_x, near_routes, normed, packed, got, part, crossed, returned, outs, rows, hidden, tail_rows,
    spread, weight,
    load_sem, gate_sem, store_sem, route_send, route_recv, x_send, x_recv, chunk_send, chunk_recv, cross_send, cross_recv,
    back_send, back_recv, pipe_send, pipe_recv,
):
    tokens, width = own_x.shape[2:]
    quarter = width // QUARTERS
    block = PARTS * HEAD
    tails = PARTS * TAIL
    pipe, place = lax.axis_index("pipe"), lax.axis_index("expert")
    y, x = place // SIDE, place % SIDE
    near = y * SIDE + x + 1 - 2 * (x % 2)
    inputs, results = (a_in, b_in), (a_out, b_out)

    def columns(q):
        return slice(q * quarter, (q + 1) * quarter)

    def partner(k, way):
        column = x + (k // SIDE) * (SIDE - 1 - 2 * x)
        return ((y + SIDE + way * (k % SIDE)) % SIDE) * SIDE + column

    def piece(k):
        if isinstance(k, int):
            return pl.ds(k * HEAD, HEAD)
        return pl.ds(pl.multiple_of(k * HEAD, HEAD), HEAD)

    def remote(source, target, send, recv, device):
        return pltpu.make_async_remote_copy(
            src_ref=source, dst_ref=target, send_sem=send, recv_sem=recv, device_id=device, device_id_type=MESH
        )

    def chunk_copy(g, h, k):
        return remote(
            packed.at[g, h, piece(k)], got.at[g, h, piece(k)], chunk_send.at[g, h, k], chunk_recv.at[g, h, k],
            (pipe, partner(k, 1)),
        )

    def back_copy(g, k):
        return remote(
            part.at[g, 0, piece(k)], returned.at[g, piece(k)], back_send.at[g, k], back_recv.at[g, k],
            (pipe, partner(k, -1)),
        )

    def cross_copy(g, k):
        return remote(
            part.at[g, 1, piece(k)], crossed.at[g, piece(k)], cross_send.at[g, k], cross_recv.at[g, k], (pipe, near)
        )

    def x_copy(s, g):
        source = inputs[g].at[0] if s == 0 else own_x.at[s, g]
        return remote(source, near_x.at[s, g], x_send.at[g], x_recv.at[g], (pipe, near))

    def route_copy():
        return remote(routes, near_routes, route_send, route_recv, (pipe, near))

    def pipe_copy(g):
        return remote(outs.at[g], own_x.at[1, g], pipe_send.at[g], pipe_recv.at[g], (pipe + 1 - 2 * g, place))

    def has_next(g):
        return pipe < pipe_count - 1 if g == 0 else pipe > 0

    def load_copy(g):
        return pltpu.make_async_copy(inputs[g].at[0], own_x.at[0, g], load_sem.at[g])

    def weight_copies(g):
        return [
            pltpu.make_async_copy(source.at[0, g], target.at[g], gate_sem.at[g, i])
            for i, (source, target) in enumerate(((gate_in, gate), (up_in, up), (down_in, down)))
        ]

    def store_copy(s, g):
        return pltpu.make_async_copy(outs.at[g], results[g].at[s, 0], store_sem.at[g])

    def later_copy():
        return pltpu.make_async_copy(later_in.at[0], own_x.at[1, 0], pipe_recv.at[0])

    def turn_copy():
        return pltpu.make_async_copy(outs.at[0], own_x.at[1, 1], pipe_recv.at[1])

    def each(first, last, action):
        lax.fori_loop(first, last, lambda k, carry: (action(k), carry)[1], 0)

    def slot_codes(chosen):
        hot = iota((PARTS, tokens), 0) == chosen
        upper = ones_where(iota((tokens, tokens), 0) <= iota((tokens, tokens), 1))
        seen = dot(ones_where(hot), upper)
        slot = jnp.sum(jnp.where(hot, seen - 1.0, 0.0), axis=0, keepdims=True)
        return chosen * 32 + slot.astype(I32)

    def selectors(codes, axis):
        shape = (block, tokens) if axis == 0 else (tokens, block)
        row = iota(shape, axis)
        k, low = row // HEAD, row % HEAD
        expert = 2 * ((y + k) % SIDE) + jnp.where(k >= SIDE, SIDE - 1 - x, x) // 2
        head = ones_where(codes == expert * 32 + low)
        tail_hit = codes == expert * 32 + HEAD + low % TAIL
        return head, [ones_where(tail_hit & (low // TAIL == q)) for q in range(QUARTERS)]

    def prepare(s, g, h):
        source = (own_x if h == 0 else near_x).at[s, g]
        gains = gain[...].astype(F32)[g:g + 1]

        def normalize(i):
            at = pl.multiple_of(i * HEAD, HEAD)
            values = source[pl.ds(at, HEAD), :].astype(F32)
            mean_square = jnp.mean(values * values, axis=-1, keepdims=True)
            scaled = (values * lax.rsqrt(mean_square + 1e-06) * gains).astype(BF16)
            for q in range(QUARTERS):
                normed[q, pl.ds(at, HEAD), :] = scaled[:, columns(q)]

        each(0, tokens // HEAD, normalize)
        chosen = (routes if h == 0 else near_routes)[2 * s + g:2 * s + g + 1, :]
        codes = slot_codes(chosen)
        head, tail = selectors(codes, 0)
        for q in range(QUARTERS):
            packed[g, h, :, columns(q)] = dot(head, normed[q]).astype(BF16)
        total = dot(tail[0], normed[0])
        for q in range(1, QUARTERS):
            total = total + dot(tail[q], normed[q])
        packed[g, h, :, width:] = total.astype(BF16)
        if h == 0:
            codes_down = jnp.transpose(jnp.broadcast_to(codes.astype(F32), (tokens, tokens))).astype(I32)
            head_down, tail_down = selectors(codes_down, 1)
            spread[g, 0] = head_down
            for q in range(QUARTERS):
                spread[g, 1 + q] = tail_down[q]
            logits = jnp.zeros((tokens, PARTS), F32)
            for q in range(QUARTERS):
                logits = logits + lax.dot_general(
                    normed[q], router[g, :, columns(q)], (((1,), (1,)), ((), ())), preferred_element_type=F32
                )
            mine = iota((tokens, PARTS), 1) == codes_down[:, :PARTS] // 32
            logit = jnp.sum(jnp.where(mine, logits, 0.0), axis=-1, keepdims=True)
            weight[g] = jnp.broadcast_to(ROUTE_GAIN * jax.nn.sigmoid(logit), (tokens, 128))

    def send_chunks(g, h):
        got[g, h, 0:HEAD, :] = packed[g, h, 0:HEAD, :]
        each(1, PARTS, lambda k: chunk_copy(g, h, k).start())

    def wait_chunks(g, h):
        each(1, PARTS, lambda k: chunk_copy(g, h, k).wait())

    def expert(g, h):
        out_row, in_row = iota((block, block), 0), iota((block, block), 1)
        gather = (out_row // TAIL % PARTS) * HEAD + (out_row // tails) * TAIL + out_row % TAIL
        scatter = (out_row % HEAD // TAIL) * tails + (out_row // HEAD) * TAIL + out_row % TAIL
        rows[0:block, :] = got[g, h, :, 0:width]
        tail = dot(ones_where(in_row == gather), got[g, h, :, width:]).astype(BF16)
        for q in range(QUARTERS):
            rows[block:, columns(q)] = tail[q * tails:(q + 1) * tails]
        units = hidden.shape[1]
        inner = min(256, units)

        def widen(j):
            at = pl.ds(pl.multiple_of(j * inner, inner), inner)
            gate_val = dot(rows[...], gate[g, :, at])
            up_val = dot(rows[...], up[g, :, at])
            hidden[:, at] = (gate_val * jax.nn.sigmoid(gate_val) * up_val).astype(BF16)

        each(0, units // inner, widen)
        step = min(512, width)

        def narrow(j):
            at = pl.ds(pl.multiple_of(j * step, step), step)
            value = dot(hidden[...], down[g, :, at]).astype(BF16)
            part[g, h, :, at] = value[:block]
            tail_rows[:, at] = value[block:]

        each(0, width // step, narrow)
        stacked = jnp.concatenate([tail_rows[:, columns(q)] for q in range(QUARTERS)], axis=0)
        part[g, h, :, width:] = dot(ones_where(in_row == scatter), stacked).astype(BF16)

    def start_cross(g):
        each(0, WINDOW, lambda k: cross_copy(g, k).start())

    def finish_cross(g, first, last):
        def one(k):
            cross_copy(g, k).wait_recv()

            @pl.when(k + WINDOW < PARTS)
            def _():
                cross_copy(g, k + WINDOW).start()

            for q in range(QUARTERS + 1):
                at = columns(q)
                total = part[g, 0, piece(k), at].astype(F32) + crossed[g, piece(k), at].astype(F32)
                part[g, 0, piece(k), at] = total.astype(BF16)

            @pl.when(k > 0)
            def _():
                back_copy(g, k).start()

            @pl.when(k == 0)
            def _():
                returned[g, 0:HEAD, :] = part[g, 0, 0:HEAD, :]

        each(first, last, one)

    def end_cross(g):
        each(0, PARTS, lambda k: cross_copy(g, k).wait_send())

    def combine(s, g):
        each(1, PARTS, lambda k: back_copy(g, k).wait())
        if s == 1:
            store_copy(0, g).wait()
            pl.when(has_next(g))(lambda: pipe_copy(g).wait_send())
        for q in range(QUARTERS):
            at = columns(q)
            expert_out = dot(spread[g, 0], returned[g, :, at]) + dot(spread[g, 1 + q], returned[g, :, width:])
            values = own_x[s, g, :, at].astype(F32)
            outs[g, :, at] = (values + weight[g, :, 0:1] * expert_out).astype(BF16)
        if s == 0:
            pl.when(has_next(g))(lambda: pipe_copy(g).start())
            if g == 0:
                pl.when(pipe == pipe_count - 1)(lambda: turn_copy().start())
        store_copy(s, g).start()

    def wait_pipe(g):
        pltpu.make_async_copy(outs.at[g], own_x.at[1, g], pipe_recv.at[g]).wait()

    for g in (0, 1):
        load_copy(g).start()
    for g in (0, 1):
        for copy in weight_copies(g):
            copy.start()
    pl.when(pipe == 0)(lambda: later_copy().start())

    barrier = pltpu.get_barrier_semaphore()

    def greet(device):
        pl.semaphore_signal(barrier, inc=1, device_id=device, device_id_type=MESH)

    each(1, PARTS, lambda k: greet((pipe, partner(k, 1))))
    greet((pipe, near))
    pl.when(pipe > 0)(lambda: greet((pipe - 1, place)))
    pl.when(pipe < pipe_count - 1)(lambda: greet((pipe + 1, place)))
    before, after = (pipe + pipe_count - 1) // pipe_count, (2 * pipe_count - 2 - pipe) // pipe_count
    pl.semaphore_wait(barrier, PARTS + before + after)

    route_copy().start()
    x_copy(0, 0).start()
    load_copy(0).wait()
    prepare(0, 0, 0)
    send_chunks(0, 0)
    load_copy(1).wait()
    prepare(0, 1, 0)
    wait_chunks(0, 0)
    send_chunks(1, 0)
    for g in (0, 1):
        for copy in weight_copies(g):
            copy.wait()
    expert(0, 0)
    route_copy().wait()

    for s in (0, 1):
        x_copy(s, 0).wait()
        x_copy(s, 1).start()
        prepare(s, 0, 1)
        send_chunks(0, 1)
        wait_chunks(1, 0)
        expert(1, 0)
        wait_chunks(0, 1)
        expert(0, 1)
        x_copy(s, 1).wait()
        start_cross(0)
        prepare(s, 1, 1)
        send_chunks(1, 1)
        finish_cross(0, 0, 4)
        wait_chunks(1, 1)
        expert(1, 1)
        finish_cross(0, 4, PARTS)
        end_cross(0)
        start_cross(1)
        combine(s, 0)
        finish_cross(1, 0, 4)
        if s == 0:
            wait_pipe(0)
            prepare(1, 0, 0)
            send_chunks(0, 0)
        finish_cross(1, 4, PARTS)
        end_cross(1)
        if s == 0:
            x_copy(1, 0).start()
        combine(s, 1)
        if s == 0:
            wait_chunks(0, 0)
            expert(0, 0)
            wait_pipe(1)
            prepare(1, 1, 0)
            send_chunks(1, 0)
    for g in (0, 1):
        store_copy(1, g).wait()


def solution(mesh):
    pipe_count = mesh.shape["pipe"]

    def body(a_init, b_init, incoming, routes, gain, router, w_gate, w_up, w_down):
        tokens, width = a_init.shape[1:]
        units = w_gate.shape[-1]
        quarter = width // QUARTERS
        long = width + quarter
        block = PARTS * HEAD
        steps = routes.shape[1]
        chosen = jnp.pad(routes.reshape(steps * 2, tokens), ((0, 8 - steps * 2), (0, 0)))
        whole = pl.BlockSpec(memory_space=pltpu.VMEM)
        outside = pl.BlockSpec(memory_space=pl.ANY)
        result = jax.ShapeDtypeStruct((steps, 1, tokens, width), BF16)
        dma = pltpu.SemaphoreType.DMA
        return pl.pallas_call(
            functools.partial(relay, pipe_count),
            out_shape=(result, result),
            in_specs=[outside] * 3 + [whole] * 3 + [outside] * 3,
            out_specs=(outside, outside),
            scratch_shapes=[
                pltpu.VMEM((2, width, units), BF16),
                pltpu.VMEM((2, width, units), BF16),
                pltpu.VMEM((2, units, width), BF16),
                pltpu.VMEM((2, 2, tokens, width), BF16),
                pltpu.VMEM((2, 2, tokens, width), BF16),
                pltpu.VMEM((8, tokens), I32),
                pltpu.VMEM((QUARTERS, tokens, quarter), BF16),
                pltpu.VMEM((2, 2, block, long), BF16),
                pltpu.VMEM((2, 2, block, long), BF16),
                pltpu.VMEM((2, 2, block, long), BF16),
                pltpu.VMEM((2, block, long), BF16),
                pltpu.VMEM((2, block, long), BF16),
                pltpu.VMEM((2, tokens, width), BF16),
                pltpu.VMEM((block + PARTS * TAIL, width), BF16),
                pltpu.VMEM((block + PARTS * TAIL, units), BF16),
                pltpu.VMEM((PARTS * TAIL, width), BF16),
                pltpu.VMEM((2, 1 + QUARTERS, tokens, block), BF16),
                pltpu.VMEM((2, tokens, 128), F32),
                dma((2,)),
                dma((2, 3)),
                dma((2,)),
                dma,
                dma,
                dma((2,)),
                dma((2,)),
                dma((2, 2, PARTS)),
                dma((2, 2, PARTS)),
                dma((2, PARTS)),
                dma((2, PARTS)),
                dma((2, PARTS)),
                dma((2, PARTS)),
                dma((2,)),
                dma((2,)),
            ],
            compiler_params=pltpu.CompilerParams(
                collective_id=0, has_side_effects=True, vmem_limit_bytes=63 * 2**20
            ),
            cost_estimate=pl.CostEstimate(
                flops=4 * 320 * width * units * 6, bytes_accessed=6 * width * units * 2 * 2, transcendentals=0
            ),
        )(a_init, b_init, incoming, chosen, gain[0], jnp.swapaxes(router[0], 1, 2), w_gate, w_up, w_down)

    placed = (
        P("pipe", "expert", None),
        P("pipe", "expert", None),
        P(None, "expert", None),
        P("pipe", None, None, "expert", None),
        P("pipe", None, None),
        P("pipe", None, None, None),
        P("pipe", None, None, "expert"),
        P("pipe", None, None, "expert"),
        P("pipe", None, "expert", None),
    )
    return jax.shard_map(
        body,
        mesh=mesh,
        in_specs=placed,
        out_specs=(P(None, "pipe", "expert", None), P(None, "pipe", "expert", None)),
        check_vma=False,
    )
```

time: 392 us -> 225 us (0.57); the launches traced: 386 us -> 225 us
  Pallas kernels: 0 us -> 219 us
  waiting for transfers between devices: 150 us -> 0 us
  starting transfers between devices: 70.2 us -> 0 us
  local copies, waits for them, and re-layouts: 68.8 us -> 5.49 us
  matrix products: 62.1 us -> 0 us
  other arithmetic: 33.7 us -> 0 us
    pallas_call x0 -> x1, Pallas kernels: none -> 219 us  [body(): pl.pallas_call(functools.partial(relay, pipe_count), out_shape=(result, r...]
    all_to_all x8 -> x0, waiting for transfers between devices: 137 us -> none  [the longest x2 43.2 us: layer_pair(): lax.all_to_all(sends[1], 'expert', split_axis=0, concat_axis=0, tiled=True)]
    all_to_all x8 -> x0, starting transfers between devices: 66.2 us -> none  [the longest x2 17.7 us: layer_pair(): lax.all_to_all(apply_expert(lax.all_to_all(sends[0], 'expert', split_axis...]
    dot_general x16 -> x0, matrix products: 62.1 us -> none  [the longest x4 31.7 us: apply_expert(): jnp.dot(hidden, down_mat, preferred_element_type=jnp.float32)]
    reshape x16 -> x0, local copies, waits for them, and re-layouts: 43.6 us -> none  [the longest x4 16.4 us: apply_expert(): return partial_value.reshape(rows.shape)]
    reduce_sum x10 -> x0, other arithmetic: 20.4 us -> none  [the longest x4 12.3 us: unpack_rows(): summed = returned.astype(jnp.float32).reshape(expert_count, copies, retur...]
    ppermute x2 -> x0, waiting for transfers between devices: 13.1 us -> none  [passed_along(): lax.ppermute(value, axis, [(source, source + steps) for source in range(l...]
    broadcast_in_dim x4 -> x0, local copies, waits for them, and re-layouts: 10.7 us -> none  [layer_pair(): sends = [jnp.repeat(packs[group], copies, axis=0) for group in (0, 1)]]
  transfers between devices with their start and end apart: 10 -> 0, of which waited for: 9 -> 0; matrix products, arithmetic and copies ran while one was open for 33% -> 0% of each run, Pallas kernels for 0% -> 0%
where the time goes in v1:
time: 225 us
  Pallas kernels  219 us (97%)
  local copies, waits for them, and re-layouts  5.49 us (2%)
    pallas_call x1, Pallas kernels, body(): pl.pallas_call(functools.partial(relay, pipe_count), out_shape=(result, r...  219 us

profile of v1, /device:TPU:100, one launch (start us, length us, event | category | flops | bytes accessed | tf_op | source)
XLA Modules:
  0.0 225.1 jit_solution(7128892732547412244)
XLA Ops:
  0.6 1.3 pad.4.routes
  1.9 218.9 %shard_map.104 = (bf16[2,1,128,3584]{3,2,1,0:T(8,128)(2,1)}, bf16[2,1,128,3584]{3,2,1,0:T(8,128)(2,1)}) custom-call(bf16[1,128,3584]{2,1,0:T(8,128)(2,1)} %a_in.1, bf16[1,128,3584]{2,1,0:T(8,128)(2,1)} %b_in.1, bf16[1,128,3584]{2,1,0:T(8,128)(2,1)} %later_in.1, s32[8,128]{1,0:T(8,128)} %pad.4.routes, bf16[2,3584]{1,0:T(2,128)(2,1)} %bitcast.7, ...), custom_call_target="tpu_custom_call" | custom-call | flops 14092861440 | bytes 44040192 | tf_op jit(solution)/shard_map/pallas_call | solution.py:344
  220.8 0.0 copy-start
  220.9 3.0 %copy.13 = bf16[2,1,128,3584]{3,2,1,0:T(8,128)(2,1)} copy(bf16[2,1,128,3584]{3,2,1,0:T(8,128)(2,1)} %get-tuple-element.4) | data formatting | bytes 3670016
  223.8 0.0 copy-done
  223.8 1.2 copy.14
Async XLA Ops:
  220.8 3.0 %copy-start = (bf16[2,1,128,3584]{3,2,1,0:T(8,128)(2,1)S(1)}, bf16[2,1,128,3584]{3,2,1,0:T(8,128)(2,1)}, u32[]{:S(2)}) copy-start(bf16[2,1,128,3584]{3,2,1,0:T(8,128)(2,1)} %get-tuple-element.5) | copy-start | bytes 5505028

commit v2 on v1

v2 whole, which is shorter than its diff:
```python
import functools

import jax
import jax.numpy as jnp
from jax import lax
from jax.experimental import pallas as pl
from jax.experimental.pallas import tpu as pltpu
from jax.sharding import PartitionSpec as P

MESH = pl.DeviceIdType.MESH
F32, BF16, I32 = jnp.float32, jnp.bfloat16, jnp.int32
ROUTE_GAIN = 2.5
SIDE = 4
PARTS = 8
HEAD, TAIL = 16, 4
LANES, CELLS = 128, 4
TILE, LONG = CELLS * LANES, CELLS * LANES + LANES


def pieces_of(width):
    tiles = width // TILE
    cuts = list(range(0, tiles, 2 if tiles > 4 else 1)) + [tiles]
    return list(zip(cuts[:-1], cuts[1:]))


def iota(shape, axis):
    return lax.broadcasted_iota(I32, shape, axis)


def ones_where(mask):
    return jnp.where(mask, 1.0, 0.0).astype(BF16)


def dot(left, right):
    return jnp.dot(left, right, preferred_element_type=F32)


ORDER = (
    ("select", 0, 0, 0), ("select", 0, 0, 1), ("weigh", 0, 0), ("own", 0, 0, 0), ("near", 0, 0, 0), ("own", 0, 0, 1),
    ("near", 0, 0, 1), ("select", 0, 1, 0), ("select", 0, 1, 1), ("near", 0, 0, 2), ("own", 0, 0, 2), ("near", 0, 0, 3),
    ("near", 0, 1, 0), ("own", 0, 1, 0), ("own", 0, 0, 3), ("expert", 0, 0, 1), ("near", 0, 1, 1), ("expert", 0, 0, 0),
    ("near", 0, 1, 2), ("finish", 0, 0, 0), ("near", 0, 1, 3), ("finish", 0, 0, 1), ("own", 0, 1, 1), ("expert", 0, 1, 1),
    ("finish", 0, 0, 2), ("combine", 0, 0, 0), ("combine", 0, 0, 1), ("own", 0, 1, 2), ("finish", 0, 0, 3), ("own", 0, 1, 3),
    ("combine", 0, 0, 2), ("combine", 0, 0, 3), ("take", 1, 0, 0), ("take", 1, 0, 1), ("select", 1, 0, 0), ("own", 1, 0, 0),
    ("weigh", 0, 1), ("own", 1, 0, 1), ("expert", 0, 1, 0), ("take", 1, 0, 2), ("take", 1, 0, 3), ("finish", 0, 1, 0),
    ("finish", 0, 1, 1), ("combine", 0, 1, 0), ("own", 1, 0, 2), ("finish", 0, 1, 2), ("select", 1, 0, 1),
    ("combine", 0, 1, 1), ("finish", 0, 1, 3), ("own", 1, 0, 3), ("near", 1, 0, 0), ("combine", 0, 1, 2), ("weigh", 1, 0),
    ("near", 1, 0, 1), ("combine", 0, 1, 3), ("take", 1, 1, 0), ("take", 1, 1, 1), ("select", 1, 1, 0), ("take", 1, 1, 2),
    ("take", 1, 1, 3), ("near", 1, 0, 2), ("own", 1, 1, 0), ("select", 1, 1, 1), ("near", 1, 0, 3), ("own", 1, 1, 1),
    ("own", 1, 1, 2), ("own", 1, 1, 3), ("expert", 1, 0, 0), ("near", 1, 1, 0), ("near", 1, 1, 1), ("expert", 1, 0, 1),
    ("expert", 1, 1, 0), ("near", 1, 1, 2), ("near", 1, 1, 3), ("finish", 1, 0, 0), ("weigh", 1, 1), ("finish", 1, 0, 1),
    ("expert", 1, 1, 1), ("finish", 1, 1, 0), ("finish", 1, 0, 2), ("finish", 1, 1, 1), ("finish", 1, 0, 3),
    ("combine", 1, 0, 0), ("combine", 1, 0, 1), ("combine", 1, 1, 0), ("combine", 1, 0, 2), ("finish", 1, 1, 2),
    ("combine", 1, 1, 1), ("finish", 1, 1, 3), ("combine", 1, 1, 2), ("combine", 1, 0, 3), ("combine", 1, 1, 3),
)


def relay(
    pipe_count,
    a_in, b_in, later_in, routes, gain, router, gate_in, up_in, down_in,
    a_out, b_out,
    gate, up, down, own_x, near_x, near_routes, normed, packed, got, part, crossed, returned, outs, rows, hidden,
    pick, spread, placed_at, weight,
    load_sem, weight_sem, store_sem, route_send, route_recv, x_send, x_recv, chunk_send, chunk_recv, cross_send, cross_recv,
    back_send, back_recv, pipe_send, pipe_recv,
):
    tokens, width = own_x.shape[2:]
    block = PARTS * HEAD
    tails = PARTS * TAIL
    tiles = width // TILE
    pieces = pieces_of(width)
    every = range(len(pieces))
    loaded = set()
    pipe, place = lax.axis_index("pipe"), lax.axis_index("expert")
    y, x = place // SIDE, place % SIDE
    near = y * SIDE + x + 1 - 2 * (x % 2)
    inputs, results = (a_in, b_in), (a_out, b_out)

    def plain(p):
        return slice(pieces[p][0] * TILE, pieces[p][1] * TILE)

    def wide(p):
        return slice(pieces[p][0] * LONG, pieces[p][1] * LONG)

    def partner(k, way):
        column = x + (k // SIDE) * (SIDE - 1 - 2 * x)
        return ((y + SIDE + way * (k % SIDE)) % SIDE) * SIDE + column

    def chunk(k):
        return pl.ds(pl.multiple_of(k * HEAD, HEAD), HEAD)

    def remote(source, target, send, recv, device):
        return pltpu.make_async_remote_copy(
            src_ref=source, dst_ref=target, send_sem=send, recv_sem=recv, device_id=device, device_id_type=MESH
        )

    def chunk_copy(g, h, p, k):
        return remote(
            packed.at[g, h, chunk(k), wide(p)], got.at[g, h, chunk(k), wide(p)],
            chunk_send.at[g, h, p, k], chunk_recv.at[g, h, p, k], (pipe, partner(k, 1)),
        )

    def back_copy(g, p, k):
        return remote(
            part.at[g, 0, chunk(k), wide(p)], returned.at[g, chunk(k), wide(p)],
            back_send.at[g, p, k], back_recv.at[g, p, k], (pipe, partner(k, -1)),
        )

    def cross_copy(g, p):
        return remote(
            part.at[g, 1, :, wide(p)], crossed.at[g, :, wide(p)], cross_send.at[g, p], cross_recv.at[g, p], (pipe, near)
        )

    def x_copy(s, g, p):
        source = inputs[g].at[0, :, plain(p)] if s == 0 else own_x.at[s, g, :, plain(p)]
        return remote(source, near_x.at[s, g, :, plain(p)], x_send.at[g, p], x_recv.at[g, p], (pipe, near))

    def route_copy():
        return remote(routes, near_routes, route_send, route_recv, (pipe, near))

    def pipe_copy(g, p):
        return remote(
            outs.at[g, :, plain(p)], own_x.at[1, g, :, plain(p)], pipe_send.at[g, p], pipe_recv.at[g, p],
            (pipe + 1 - 2 * g, place),
        )

    def has_next(g):
        return pipe < pipe_count - 1 if g == 0 else pipe > 0

    def load_copy(g):
        return pltpu.make_async_copy(inputs[g].at[0], own_x.at[0, g], load_sem.at[g])

    def weight_copies(g):
        return [
            pltpu.make_async_copy(source.at[0, g], target.at[g], weight_sem.at[g, i])
            for i, (source, target) in enumerate(((gate_in, gate), (up_in, up), (down_in, down)))
        ]

    def store_copy(s, g, p):
        return pltpu.make_async_copy(outs.at[g, :, plain(p)], results[g].at[s, 0, :, plain(p)], store_sem.at[g, p])

    def later_copy(p):
        return pltpu.make_async_copy(later_in.at[0, :, plain(p)], own_x.at[1, 0, :, plain(p)], pipe_recv.at[0, p])

    def turn_copy(p):
        return pltpu.make_async_copy(outs.at[0, :, plain(p)], own_x.at[1, 1, :, plain(p)], pipe_recv.at[1, p])

    def each(first, last, action):
        lax.fori_loop(first, last, lambda k, carry: (action(k), carry)[1], 0)

    def slot_codes(chosen):
        hot = iota((PARTS, tokens), 0) == chosen
        upper = ones_where(iota((tokens, tokens), 0) <= iota((tokens, tokens), 1))
        seen = dot(ones_where(hot), upper)
        slot = jnp.sum(jnp.where(hot, seen - 1.0, 0.0), axis=0, keepdims=True)
        return chosen * 32 + slot.astype(I32)

    def selectors(codes, axis):
        shape = (block, tokens) if axis == 0 else (tokens, block)
        row = iota(shape, axis)
        k, low = row // HEAD, row % HEAD
        expert = 2 * ((y + k) % SIDE) + jnp.where(k >= SIDE, SIDE - 1 - x, x) // 2
        tail_hit = codes == expert * 32 + HEAD + low % TAIL
        return [ones_where(codes == expert * 32 + low)] + [ones_where(tail_hit & (low // TAIL == b)) for b in range(CELLS)]

    def select(s, g, h):
        chosen = (routes if h == 0 else near_routes)[2 * s + g:2 * s + g + 1, :]
        codes = slot_codes(chosen)
        for i, selector in enumerate(selectors(codes, 0)):
            pick[g, h, i] = selector
        if h == 0:
            codes_down = jnp.transpose(jnp.broadcast_to(codes.astype(F32), (tokens, tokens))).astype(I32)
            placed_at[g] = codes_down
            for i, selector in enumerate(selectors(codes_down, 1)):
                spread[g, i] = selector

    def normalize(source, target, gains, count):
        def one(i):
            at = pl.ds(pl.multiple_of(i * HEAD, HEAD), HEAD)
            values = source[at, :].astype(F32)
            mean_square = jnp.mean(values * values, axis=-1, keepdims=True)
            target[at, :] = (values * lax.rsqrt(mean_square + 1e-06) * gains).astype(BF16)

        each(0, count // HEAD, one)

    def weigh(s, g):
        normalize(own_x.at[s, g], normed, gain[...].astype(F32)[g:g + 1], tokens)
        logits = lax.dot_general(normed[...], router[g], (((1,), (1,)), ((), ())), preferred_element_type=F32)
        mine = iota((tokens, PARTS), 1) == placed_at[g, :, 0:PARTS] // 32
        logit = jnp.sum(jnp.where(mine, logits, 0.0), axis=-1, keepdims=True)
        weight[g] = jnp.broadcast_to(ROUTE_GAIN * jax.nn.sigmoid(logit), (tokens, LANES))

    def send_piece(s, g, h, p):
        source = (own_x if h == 0 else near_x).at[s, g]
        for c in range(*pieces[p]):
            values = source[:, c * TILE:(c + 1) * TILE]
            packed[g, h, :, c * LONG:c * LONG + TILE] = dot(pick[g, h, 0], values).astype(BF16)
            total = dot(pick[g, h, 1], values[:, :LANES])
            for b in range(1, CELLS):
                total = total + dot(pick[g, h, 1 + b], values[:, b * LANES:(b + 1) * LANES])
            packed[g, h, :, c * LONG + TILE:(c + 1) * LONG] = total.astype(BF16)
        each(1, PARTS, lambda k: chunk_copy(g, h, p, k).start())
        got[g, h, 0:HEAD, wide(p)] = packed[g, h, 0:HEAD, wide(p)]

    def send_own(s, g, p):
        send_piece(s, g, 0, p)

    def send_near(s, g, p):
        x_copy(s, g, p).wait()
        send_piece(s, g, 1, p)

    def wait_chunks(g, h):
        for p in every:
            each(1, PARTS, lambda k: chunk_copy(g, h, p, k).wait())

    def expert(s, g, h):
        if g not in loaded:
            loaded.add(g)
            for copy in weight_copies(g):
                copy.wait()
        wait_chunks(g, h)
        out_row, in_row = iota((block, block), 0), iota((block, block), 1)
        gather = (out_row // TAIL % PARTS) * HEAD + (out_row // tails) * TAIL + out_row % TAIL
        scatter = ones_where(in_row == (out_row % HEAD // TAIL) * tails + (out_row // HEAD) * TAIL + out_row % TAIL)
        for c in range(tiles):
            rows[0:block, c * TILE:(c + 1) * TILE] = got[g, h, :, c * LONG:c * LONG + TILE]
        cells = jnp.concatenate([got[g, h, :, c * LONG + TILE:(c + 1) * LONG] for c in range(tiles)], axis=1)
        cells = dot(ones_where(in_row == gather), cells).astype(BF16)
        for c in range(tiles):
            for b in range(CELLS):
                at = c * TILE + b * LANES
                rows[block:, at:at + LANES] = cells[b * tails:(b + 1) * tails, c * LANES:(c + 1) * LANES]
        normalize(rows, rows, gain[...].astype(F32)[g:g + 1], block + tails)
        units = hidden.shape[1]
        inner = min(256, units)

        def widen(j):
            at = pl.ds(pl.multiple_of(j * inner, inner), inner)
            gate_val = dot(rows[...], gate[g, :, at])
            up_val = dot(rows[...], up[g, :, at])
            hidden[:, at] = (gate_val * jax.nn.sigmoid(gate_val) * up_val).astype(BF16)

        each(0, units // inner, widen)

        def narrow(c):
            value = dot(hidden[...], down[g, :, pl.ds(pl.multiple_of(c * TILE, TILE), TILE)]).astype(BF16)
            part[g, h, :, pl.ds(pl.multiple_of(c * LONG, LANES), TILE)] = value[:block]
            stacked = jnp.concatenate([value[block:, b * LANES:(b + 1) * LANES] for b in range(CELLS)], axis=0)
            part[g, h, :, pl.ds(pl.multiple_of(c * LONG + TILE, LANES), LANES)] = dot(scatter, stacked).astype(BF16)

        for p in every:
            each(*pieces[p], narrow)
            if h == 1:
                cross_copy(g, p).start()

    def finish_cross(s, g, p):
        cross_copy(g, p).wait()
        for c in range(*pieces[p]):
            at = slice(c * LONG, (c + 1) * LONG)
            part[g, 0, :, at] = (part[g, 0, :, at].astype(F32) + crossed[g, :, at].astype(F32)).astype(BF16)
        each(1, PARTS, lambda k: back_copy(g, p, k).start())
        returned[g, 0:HEAD, wide(p)] = part[g, 0, 0:HEAD, wide(p)]

    def combine(s, g, p):
        each(1, PARTS, lambda k: back_copy(g, p, k).wait())
        if s == 1:
            store_copy(0, g, p).wait()
            pl.when(has_next(g))(lambda: pipe_copy(g, p).wait_send())
        for c in range(*pieces[p]):
            at = slice(c * TILE, (c + 1) * TILE)
            cells = returned[g, :, c * LONG + TILE:(c + 1) * LONG]
            expert_out = dot(spread[g, 0], returned[g, :, c * LONG:c * LONG + TILE])
            expert_out = expert_out + jnp.concatenate([dot(spread[g, 1 + b], cells) for b in range(CELLS)], axis=1)
            values = own_x[s, g, :, at].astype(F32)
            outs[g, :, at] = (values + weight[g, :, 0:1] * expert_out).astype(BF16)
        if s == 0:
            pl.when(has_next(g))(lambda: pipe_copy(g, p).start())
            if g == 0:
                pl.when(pipe == pipe_count - 1)(lambda: turn_copy(p).start())
        store_copy(s, g, p).start()

    def take(s, g, p):
        pltpu.make_async_copy(outs.at[g, :, plain(p)], own_x.at[s, g, :, plain(p)], pipe_recv.at[g, p]).wait()
        x_copy(s, g, p).start()

    for g in (0, 1):
        load_copy(g).start()
    for g in (0, 1):
        for copy in weight_copies(g):
            copy.start()

    @pl.when(pipe == 0)
    def _():
        for p in every:
            later_copy(p).start()

    barrier = pltpu.get_barrier_semaphore()

    def greet(device):
        pl.semaphore_signal(barrier, inc=1, device_id=device, device_id_type=MESH)

    each(1, PARTS, lambda k: greet((pipe, partner(k, 1))))
    greet((pipe, near))
    pl.when(pipe > 0)(lambda: greet((pipe - 1, place)))
    pl.when(pipe < pipe_count - 1)(lambda: greet((pipe + 1, place)))
    before, after = (pipe + pipe_count - 1) // pipe_count, (2 * pipe_count - 2 - pipe) // pipe_count
    pl.semaphore_wait(barrier, PARTS + before + after)

    route_copy().start()
    for g in (0, 1):
        for p in every:
            x_copy(0, g, p).start()
    route_copy().wait()
    for g in (0, 1):
        load_copy(g).wait()
    actions = dict(
        select=select, own=send_own, near=send_near, take=take, weigh=weigh, expert=expert, finish=finish_cross, combine=combine
    )
    for name, *where in ORDER:
        actions[name](*where)
    for g in (0, 1):
        for p in every:
            store_copy(1, g, p).wait()


def solution(mesh):
    pipe_count = mesh.shape["pipe"]

    def body(a_init, b_init, incoming, routes, gain, router, w_gate, w_up, w_down):
        tokens, width = a_init.shape[1:]
        units = w_gate.shape[-1]
        long = width // TILE * LONG
        block = PARTS * HEAD
        count = len(pieces_of(width))
        steps = routes.shape[1]
        chosen = routes.reshape(steps * 2, tokens)
        whole = pl.BlockSpec(memory_space=pltpu.VMEM)
        outside = pl.BlockSpec(memory_space=pl.ANY)
        result = jax.ShapeDtypeStruct((steps, 1, tokens, width), BF16)
        dma = pltpu.SemaphoreType.DMA
        return pl.pallas_call(
            functools.partial(relay, pipe_count),
            out_shape=(result, result),
            in_specs=[outside] * 3 + [whole] * 3 + [outside] * 3,
            out_specs=(outside, outside),
            scratch_shapes=[
                pltpu.VMEM((2, width, units), BF16),
                pltpu.VMEM((2, width, units), BF16),
                pltpu.VMEM((2, units, width), BF16),
                pltpu.VMEM((2, 2, tokens, width), BF16),
                pltpu.VMEM((2, 2, tokens, width), BF16),
                pltpu.VMEM((steps * 2, tokens), I32),
                pltpu.VMEM((tokens, width), BF16),
                pltpu.VMEM((2, 2, block, long), BF16),
                pltpu.VMEM((2, 2, block, long), BF16),
                pltpu.VMEM((2, 2, block, long), BF16),
                pltpu.VMEM((2, block, long), BF16),
                pltpu.VMEM((2, block, long), BF16),
                pltpu.VMEM((2, tokens, width), BF16),
                pltpu.VMEM((block + PARTS * TAIL, width), BF16),
                pltpu.VMEM((block + PARTS * TAIL, units), BF16),
                pltpu.VMEM((2, 2, 1 + CELLS, block, tokens), BF16),
                pltpu.VMEM((2, 1 + CELLS, tokens, block), BF16),
                pltpu.VMEM((2, tokens, tokens), I32),
                pltpu.VMEM((2, tokens, LANES), F32),
                dma((2,)),
                dma((2, 3)),
                dma((2, count)),
                dma,
                dma,
                dma((2, count)),
                dma((2, count)),
                dma((2, 2, count, PARTS)),
                dma((2, 2, count, PARTS)),
                dma((2, count)),
                dma((2, count)),
                dma((2, count, PARTS)),
                dma((2, count, PARTS)),
                dma((2, count)),
                dma((2, count)),
            ],
            compiler_params=pltpu.CompilerParams(
                collective_id=0, has_side_effects=True, vmem_limit_bytes=63 * 2**20
            ),
            cost_estimate=pl.CostEstimate(
                flops=4 * 320 * width * units * 6, bytes_accessed=6 * width * units * 2 * 2, transcendentals=0
            ),
        )(a_init, b_init, incoming, chosen, gain[0], jnp.swapaxes(router[0], 1, 2), w_gate, w_up, w_down)

    placed = (
        P("pipe", "expert", None),
        P("pipe", "expert", None),
        P(None, "expert", None),
        P("pipe", None, None, "expert", None),
        P("pipe", None, None),
        P("pipe", None, None, None),
        P("pipe", None, None, "expert"),
        P("pipe", None, None, "expert"),
        P("pipe", None, "expert", None),
    )
    return jax.shard_map(
        body,
        mesh=mesh,
        in_specs=placed,
        out_specs=(P(None, "pipe", "expert", None), P(None, "pipe", "expert", None)),
        check_vma=False,
    )
```

time: 225 us -> 201 us (0.89); the launches traced: 225 us -> 198 us
  Pallas kernels: 219 us -> 194 us
    pallas_call x1, Pallas kernels: 219 us -> 194 us  [body(): pl.pallas_call(functools.partial(relay, pipe_count), out_shape=(result, r...]
where the time goes in v2:
time: 201 us; the launch traced here: 198 us
  Pallas kernels  194 us (97%)
  local copies, waits for them, and re-layouts  4.21 us (2%)
    pallas_call x1, Pallas kernels, body(): pl.pallas_call(functools.partial(relay, pipe_count), out_shape=(result, r...  194 us
    unnamed x4, local copies, waits for them, and re-layouts  4.21 us

profile of v2, /device:TPU:100, one launch (start us, length us, event | category | flops | bytes accessed | tf_op | source)
XLA Modules:
  0.0 198.4 jit_solution(3635364151168106283)
XLA Ops:
  0.6 193.5 %shard_map.104 = (bf16[2,1,128,3584]{3,2,1,0:T(8,128)(2,1)}, bf16[2,1,128,3584]{3,2,1,0:T(8,128)(2,1)}) custom-call(bf16[1,128,3584]{2,1,0:T(8,128)(2,1)} %a_in.1, bf16[1,128,3584]{2,1,0:T(8,128)(2,1)} %b_in.1, bf16[1,128,3584]{2,1,0:T(8,128)(2,1)} %later_in.1, s32[4,128]{1,0:T(4,128)} %bitcast.7, bf16[2,3584]{1,0:T(2,128)(2,1)} %bitcast.6, ...), custom_call_target="tpu_custom_call" | custom-call | flops 14092861440 | bytes 44040192 | tf_op jit(solution)/shard_map/pallas_call | solution.py:341
  194.1 0.0 copy-start
  194.2 3.0 %copy.13 = bf16[2,1,128,3584]{3,2,1,0:T(8,128)(2,1)} copy(bf16[2,1,128,3584]{3,2,1,0:T(8,128)(2,1)} %get-tuple-element.4) | data formatting | bytes 3670016
  197.1 0.0 copy-done
  197.1 1.2 copy.14
Async XLA Ops:
  194.1 3.0 %copy-start = (bf16[2,1,128,3584]{3,2,1,0:T(8,128)(2,1)S(1)}, bf16[2,1,128,3584]{3,2,1,0:T(8,128)(2,1)}, u32[]{:S(2)}) copy-start(bf16[2,1,128,3584]{3,2,1,0:T(8,128)(2,1)} %get-tuple-element.5) | copy-start | bytes 5505028

commit v3 on v2

--- a/solution.py
+++ b/solution.py
@@ -23,6 +23,9 @@
     return list(zip(cuts[:-1], cuts[1:]))
 
 
+DIRECT = 2
+
+
 def iota(shape, axis):
     return lax.broadcasted_iota(I32, shape, axis)
 
@@ -36,22 +39,22 @@
 
 
 ORDER = (
-    ("select", 0, 0, 0), ("select", 0, 0, 1), ("weigh", 0, 0), ("own", 0, 0, 0), ("near", 0, 0, 0), ("own", 0, 0, 1),
-    ("near", 0, 0, 1), ("select", 0, 1, 0), ("select", 0, 1, 1), ("near", 0, 0, 2), ("own", 0, 0, 2), ("near", 0, 0, 3),
-    ("near", 0, 1, 0), ("own", 0, 1, 0), ("own", 0, 0, 3), ("expert", 0, 0, 1), ("near", 0, 1, 1), ("expert", 0, 0, 0),
-    ("near", 0, 1, 2), ("finish", 0, 0, 0), ("near", 0, 1, 3), ("finish", 0, 0, 1), ("own", 0, 1, 1), ("expert", 0, 1, 1),
-    ("finish", 0, 0, 2), ("combine", 0, 0, 0), ("combine", 0, 0, 1), ("own", 0, 1, 2), ("finish", 0, 0, 3), ("own", 0, 1, 3),
-    ("combine", 0, 0, 2), ("combine", 0, 0, 3), ("take", 1, 0, 0), ("take", 1, 0, 1), ("select", 1, 0, 0), ("own", 1, 0, 0),
-    ("weigh", 0, 1), ("own", 1, 0, 1), ("expert", 0, 1, 0), ("take", 1, 0, 2), ("take", 1, 0, 3), ("finish", 0, 1, 0),
-    ("finish", 0, 1, 1), ("combine", 0, 1, 0), ("own", 1, 0, 2), ("finish", 0, 1, 2), ("select", 1, 0, 1),
-    ("combine", 0, 1, 1), ("finish", 0, 1, 3), ("own", 1, 0, 3), ("near", 1, 0, 0), ("combine", 0, 1, 2), ("weigh", 1, 0),
-    ("near", 1, 0, 1), ("combine", 0, 1, 3), ("take", 1, 1, 0), ("take", 1, 1, 1), ("select", 1, 1, 0), ("take", 1, 1, 2),
-    ("take", 1, 1, 3), ("near", 1, 0, 2), ("own", 1, 1, 0), ("select", 1, 1, 1), ("near", 1, 0, 3), ("own", 1, 1, 1),
-    ("own", 1, 1, 2), ("own", 1, 1, 3), ("expert", 1, 0, 0), ("near", 1, 1, 0), ("near", 1, 1, 1), ("expert", 1, 0, 1),
-    ("expert", 1, 1, 0), ("near", 1, 1, 2), ("near", 1, 1, 3), ("finish", 1, 0, 0), ("weigh", 1, 1), ("finish", 1, 0, 1),
-    ("expert", 1, 1, 1), ("finish", 1, 1, 0), ("finish", 1, 0, 2), ("finish", 1, 1, 1), ("finish", 1, 0, 3),
-    ("combine", 1, 0, 0), ("combine", 1, 0, 1), ("combine", 1, 1, 0), ("combine", 1, 0, 2), ("finish", 1, 1, 2),
-    ("combine", 1, 1, 1), ("finish", 1, 1, 3), ("combine", 1, 1, 2), ("combine", 1, 0, 3), ("combine", 1, 1, 3),
+    ("select", 0, 1, 0), ("own", 0, 1, 0), ("select", 0, 0, 0), ("own", 0, 0, 0), ("select", 0, 0, 1), ("own", 0, 0, 1),
+    ("near", 0, 0, 0), ("own", 0, 1, 1), ("near", 0, 0, 1), ("own", 0, 0, 2), ("near", 0, 0, 2), ("near", 0, 0, 3),
+    ("own", 0, 1, 2), ("own", 0, 0, 3), ("select", 0, 1, 1), ("near", 0, 1, 0), ("weigh", 0, 1), ("expert", 0, 0, 1),
+    ("near", 0, 1, 1), ("weigh", 0, 0), ("turn", 0, 0, 2), ("near", 0, 1, 2), ("near", 0, 1, 3), ("expert", 0, 0, 0),
+    ("turn", 0, 0, 3), ("finish", 0, 0, 0), ("own", 0, 1, 3), ("finish", 0, 0, 1), ("expert", 0, 1, 1), ("expert", 0, 1, 0),
+    ("combine", 0, 0, 0), ("combine", 0, 0, 1), ("finish", 0, 1, 0), ("turn", 0, 1, 2), ("combine", 0, 0, 2),
+    ("combine", 0, 0, 3), ("select", 1, 0, 1), ("turn", 0, 1, 3), ("take", 1, 0, 0), ("finish", 0, 1, 1), ("select", 1, 0, 0),
+    ("combine", 0, 1, 0), ("own", 1, 0, 0), ("take", 1, 0, 1), ("own", 1, 0, 1), ("take", 1, 0, 2), ("combine", 0, 1, 1),
+    ("own", 1, 0, 2), ("take", 1, 0, 3), ("combine", 0, 1, 2), ("own", 1, 0, 3), ("combine", 0, 1, 3), ("take", 1, 1, 0),
+    ("near", 1, 0, 0), ("take", 1, 1, 1), ("select", 1, 1, 0), ("own", 1, 1, 0), ("near", 1, 0, 1), ("weigh", 1, 0),
+    ("near", 1, 0, 2), ("near", 1, 0, 3), ("take", 1, 1, 2), ("expert", 1, 0, 0), ("take", 1, 1, 3), ("select", 1, 1, 1),
+    ("own", 1, 1, 1), ("near", 1, 1, 0), ("near", 1, 1, 1), ("expert", 1, 0, 1), ("near", 1, 1, 2), ("turn", 1, 0, 2),
+    ("near", 1, 1, 3), ("turn", 1, 0, 3), ("own", 1, 1, 2), ("finish", 1, 0, 0), ("own", 1, 1, 3), ("expert", 1, 1, 1),
+    ("finish", 1, 0, 1), ("expert", 1, 1, 0), ("turn", 1, 1, 2), ("combine", 1, 0, 0), ("turn", 1, 1, 3), ("finish", 1, 1, 0),
+    ("combine", 1, 0, 1), ("combine", 1, 0, 2), ("finish", 1, 1, 1), ("weigh", 1, 1), ("combine", 1, 0, 3),
+    ("combine", 1, 1, 0), ("combine", 1, 1, 1), ("combine", 1, 1, 2), ("combine", 1, 1, 3),
 )
 
 
@@ -59,10 +62,10 @@
     pipe_count,
     a_in, b_in, later_in, routes, gain, router, gate_in, up_in, down_in,
     a_out, b_out,
-    gate, up, down, own_x, near_x, near_routes, normed, packed, got, part, crossed, returned, outs, rows, hidden,
-    pick, spread, placed_at, weight,
+    gate, up, down, own_x, near_x, near_routes, normed, packed, got, part, crossed, returned, near_returned, turned, met, outs, rows, hidden,
+    pick, spread, near_spread, placed_at, weight,
     load_sem, weight_sem, store_sem, route_send, route_recv, x_send, x_recv, chunk_send, chunk_recv, cross_send, cross_recv,
-    back_send, back_recv, pipe_send, pipe_recv,
+    back_send, back_recv, near_back_send, near_back_recv, turn_send, turn_recv, pipe_send, pipe_recv,
 ):
     tokens, width = own_x.shape[2:]
     block = PARTS * HEAD
@@ -82,6 +85,14 @@
     def wide(p):
         return slice(pieces[p][0] * LONG, pieces[p][1] * LONG)
 
+    first_direct = pieces[DIRECT][0]
+
+    def late(p):
+        return slice((pieces[p][0] - first_direct) * TILE, (pieces[p][1] - first_direct) * TILE)
+
+    def late_wide(p):
+        return slice((pieces[p][0] - first_direct) * LONG, (pieces[p][1] - first_direct) * LONG)
+
     def partner(k, way):
         column = x + (k // SIDE) * (SIDE - 1 - 2 * x)
         return ((y + SIDE + way * (k % SIDE)) % SIDE) * SIDE + column
@@ -104,6 +115,18 @@
         return remote(
             part.at[g, 0, chunk(k), wide(p)], returned.at[g, chunk(k), wide(p)],
             back_send.at[g, p, k], back_recv.at[g, p, k], (pipe, partner(k, -1)),
+        )
+
+    def near_back_copy(g, p, k):
+        return remote(
+            part.at[g, 1, chunk(k), wide(p)], near_returned.at[g, chunk(k), late_wide(p)],
+            near_back_send.at[g, p - DIRECT, k], near_back_recv.at[g, p - DIRECT, k], (pipe, partner(k, -1)),
+        )
+
+    def turned_copy(g, p):
+        return remote(
+            turned.at[g, :, late(p)], met.at[g, :, late(p)], turn_send.at[g, p - DIRECT], turn_recv.at[g, p - DIRECT],
+            (pipe, near),
         )
 
     def cross_copy(g, p):
@@ -168,11 +191,12 @@
         codes = slot_codes(chosen)
         for i, selector in enumerate(selectors(codes, 0)):
             pick[g, h, i] = selector
+        codes_down = jnp.transpose(jnp.broadcast_to(codes.astype(F32), (tokens, tokens))).astype(I32)
+        target = spread if h == 0 else near_spread
+        for i, selector in enumerate(selectors(codes_down, 1)):
+            target[g, i] = selector
         if h == 0:
-            codes_down = jnp.transpose(jnp.broadcast_to(codes.astype(F32), (tokens, tokens))).astype(I32)
             placed_at[g] = codes_down
-            for i, selector in enumerate(selectors(codes_down, 1)):
-                spread[g, i] = selector
 
     def normalize(source, target, gains, count):
         def one(i):
@@ -212,6 +236,10 @@
     def wait_chunks(g, h):
         for p in every:
             each(1, PARTS, lambda k: chunk_copy(g, h, p, k).wait())
+
+    def send_back(g, p):
+        each(1, PARTS, lambda k: back_copy(g, p, k).start())
+        returned[g, 0:HEAD, wide(p)] = part[g, 0, 0:HEAD, wide(p)]
 
     def expert(s, g, h):
         if g not in loaded:
@@ -250,7 +278,12 @@
 
         for p in every:
             each(*pieces[p], narrow)
-            if h == 1:
+            if p >= DIRECT and h == 1:
+                each(1, PARTS, lambda k: near_back_copy(g, p, k).start())
+                near_returned[g, 0:HEAD, late_wide(p)] = part[g, 1, 0:HEAD, wide(p)]
+            elif p >= DIRECT:
+                send_back(g, p)
+            elif h == 1:
                 cross_copy(g, p).start()
 
     def finish_cross(s, g, p):
@@ -258,19 +291,33 @@
         for c in range(*pieces[p]):
             at = slice(c * LONG, (c + 1) * LONG)
             part[g, 0, :, at] = (part[g, 0, :, at].astype(F32) + crossed[g, :, at].astype(F32)).astype(BF16)
-        each(1, PARTS, lambda k: back_copy(g, p, k).start())
-        returned[g, 0:HEAD, wide(p)] = part[g, 0, 0:HEAD, wide(p)]
+        send_back(g, p)
+
+    def gathered(selector, source, at):
+        cells = source[:, at + TILE:at + LONG]
+        tail = jnp.concatenate([dot(selector[1 + b], cells) for b in range(CELLS)], axis=1)
+        return dot(selector[0], source[:, at:at + TILE]) + tail
+
+    def turn(s, g, p):
+        each(1, PARTS, lambda k: near_back_copy(g, p, k).wait())
+        for c in range(*pieces[p]):
+            i = c - first_direct
+            values = gathered(near_spread.at[g], near_returned.at[g], i * LONG)
+            turned[g, :, i * TILE:(i + 1) * TILE] = values.astype(BF16)
+        turned_copy(g, p).start()
 
     def combine(s, g, p):
         each(1, PARTS, lambda k: back_copy(g, p, k).wait())
+        if p >= DIRECT:
+            turned_copy(g, p).wait()
         if s == 1:
             store_copy(0, g, p).wait()
             pl.when(has_next(g))(lambda: pipe_copy(g, p).wait_send())
         for c in range(*pieces[p]):
             at = slice(c * TILE, (c + 1) * TILE)
-            cells = returned[g, :, c * LONG + TILE:(c + 1) * LONG]
-            expert_out = dot(spread[g, 0], returned[g, :, c * LONG:c * LONG + TILE])
-            expert_out = expert_out + jnp.concatenate([dot(spread[g, 1 + b], cells) for b in range(CELLS)], axis=1)
+            expert_out = gathered(spread.at[g], returned.at[g], c * LONG)
+            if p >= DIRECT:
+                expert_out = expert_out + met[g, :, (c - first_direct) * TILE:(c - first_direct + 1) * TILE].astype(F32)
             values = own_x[s, g, :, at].astype(F32)
             outs[g, :, at] = (values + weight[g, :, 0:1] * expert_out).astype(BF16)
         if s == 0:
@@ -314,7 +361,8 @@
     for g in (0, 1):
         load_copy(g).wait()
     actions = dict(
-        select=select, own=send_own, near=send_near, take=take, weigh=weigh, expert=expert, finish=finish_cross, combine=combine
+        select=select, own=send_own, near=send_near, take=take, weigh=weigh, expert=expert, finish=finish_cross, turn=turn,
+        combine=combine,
     )
     for name, *where in ORDER:
         actions[name](*where)
@@ -331,7 +379,9 @@
         units = w_gate.shape[-1]
         long = width // TILE * LONG
         block = PARTS * HEAD
-        count = len(pieces_of(width))
+        pieces = pieces_of(width)
+        count = len(pieces)
+        late_tiles = width // TILE - pieces[DIRECT][0]
         steps = routes.shape[1]
         chosen = routes.reshape(steps * 2, tokens)
         whole = pl.BlockSpec(memory_space=pltpu.VMEM)
@@ -356,11 +406,15 @@
                 pltpu.VMEM((2, 2, block, long), BF16),
                 pltpu.VMEM((2, block, long), BF16),
                 pltpu.VMEM((2, block, long), BF16),
+                pltpu.VMEM((2, block, late_tiles * LONG), BF16),
+                pltpu.VMEM((2, tokens, late_tiles * TILE), BF16),
+                pltpu.VMEM((2, tokens, late_tiles * TILE), BF16),
                 pltpu.VMEM((2, tokens, width), BF16),
                 pltpu.VMEM((block + PARTS * TAIL, width), BF16),
                 pltpu.VMEM((block + PARTS * TAIL, units), BF16),
                 pltpu.VMEM((2, 2, 1 + CELLS, block, tokens), BF16),
                 pltpu.VMEM((2, 1 + CELLS, tokens, block), BF16),
+                pltpu.VMEM((2, 1 + CELLS, tokens, block), BF16),
                 pltpu.VMEM((2, tokens, tokens), I32),
                 pltpu.VMEM((2, tokens, LANES), F32),
                 dma((2,)),
@@ -376,6 +430,10 @@
                 dma((2, count)),
                 dma((2, count, PARTS)),
                 dma((2, count, PARTS)),
+                dma((2, count - DIRECT, PARTS)),
+                dma((2, count - DIRECT, PARTS)),
+                dma((2, count - DIRECT)),
+                dma((2, count - DIRECT)),
                 dma((2, count)),
                 dma((2, count)),
             ],

time: 201 us -> 192 us (0.955)
  Pallas kernels: 194 us -> 186 us
    pallas_call x1, Pallas kernels: 194 us -> 186 us  [body(): pl.pallas_call(functools.partial(relay, pipe_count), out_shape=(result, r...]
where the time goes in v3:
time: 192 us; the launch traced here: 190 us
  Pallas kernels  186 us (97%)
  local copies, waits for them, and re-layouts  4.21 us (2%)
    pallas_call x1, Pallas kernels, body(): pl.pallas_call(functools.partial(relay, pipe_count), out_shape=(result, r...  186 us
    unnamed x4, local copies, waits for them, and re-layouts  4.21 us

profile of v3, /device:TPU:100, one launch (start us, length us, event | category | flops | bytes accessed | tf_op | source)
XLA Modules:
  0.0 190.5 jit_solution(12057585936997201960)
XLA Ops:
  0.6 185.6 %shard_map.104 = (bf16[2,1,128,3584]{3,2,1,0:T(8,128)(2,1)}, bf16[2,1,128,3584]{3,2,1,0:T(8,128)(2,1)}) custom-call(bf16[1,128,3584]{2,1,0:T(8,128)(2,1)} %a_in.1, bf16[1,128,3584]{2,1,0:T(8,128)(2,1)} %b_in.1, bf16[1,128,3584]{2,1,0:T(8,128)(2,1)} %later_in.1, s32[4,128]{1,0:T(4,128)} %bitcast.7, bf16[2,3584]{1,0:T(2,128)(2,1)} %bitcast.6, ...), custom_call_target="tpu_custom_call" | custom-call | flops 14092861440 | bytes 44040192 | tf_op jit(solution)/shard_map/pallas_call | solution.py:391
  186.2 0.0 copy-start
  186.2 3.0 %copy.13 = bf16[2,1,128,3584]{3,2,1,0:T(8,128)(2,1)} copy(bf16[2,1,128,3584]{3,2,1,0:T(8,128)(2,1)} %get-tuple-element.4) | data formatting | bytes 3670016
  189.2 0.0 copy-done
  189.2 1.2 copy.14
Async XLA Ops:
  186.2 3.0 %copy-start = (bf16[2,1,128,3584]{3,2,1,0:T(8,128)(2,1)S(1)}, bf16[2,1,128,3584]{3,2,1,0:T(8,128)(2,1)}, u32[]{:S(2)}) copy-start(bf16[2,1,128,3584]{3,2,1,0:T(8,128)(2,1)} %get-tuple-element.5) | copy-start | bytes 5505028

commit v4 on v3

--- a/solution.py
+++ b/solution.py
@@ -19,10 +19,11 @@
 
 def pieces_of(width):
     tiles = width // TILE
-    cuts = list(range(0, tiles, 2 if tiles > 4 else 1)) + [tiles]
+    cuts = [cut for cut in CUTS if cut < tiles] + [tiles]
     return list(zip(cuts[:-1], cuts[1:]))
 
 
+CUTS = (0, 3, 5)
 DIRECT = 2
 
 
@@ -39,22 +40,19 @@
 
 
 ORDER = (
-    ("select", 0, 1, 0), ("own", 0, 1, 0), ("select", 0, 0, 0), ("own", 0, 0, 0), ("select", 0, 0, 1), ("own", 0, 0, 1),
-    ("near", 0, 0, 0), ("own", 0, 1, 1), ("near", 0, 0, 1), ("own", 0, 0, 2), ("near", 0, 0, 2), ("near", 0, 0, 3),
-    ("own", 0, 1, 2), ("own", 0, 0, 3), ("select", 0, 1, 1), ("near", 0, 1, 0), ("weigh", 0, 1), ("expert", 0, 0, 1),
-    ("near", 0, 1, 1), ("weigh", 0, 0), ("turn", 0, 0, 2), ("near", 0, 1, 2), ("near", 0, 1, 3), ("expert", 0, 0, 0),
-    ("turn", 0, 0, 3), ("finish", 0, 0, 0), ("own", 0, 1, 3), ("finish", 0, 0, 1), ("expert", 0, 1, 1), ("expert", 0, 1, 0),
-    ("combine", 0, 0, 0), ("combine", 0, 0, 1), ("finish", 0, 1, 0), ("turn", 0, 1, 2), ("combine", 0, 0, 2),
-    ("combine", 0, 0, 3), ("select", 1, 0, 1), ("turn", 0, 1, 3), ("take", 1, 0, 0), ("finish", 0, 1, 1), ("select", 1, 0, 0),
-    ("combine", 0, 1, 0), ("own", 1, 0, 0), ("take", 1, 0, 1), ("own", 1, 0, 1), ("take", 1, 0, 2), ("combine", 0, 1, 1),
-    ("own", 1, 0, 2), ("take", 1, 0, 3), ("combine", 0, 1, 2), ("own", 1, 0, 3), ("combine", 0, 1, 3), ("take", 1, 1, 0),
-    ("near", 1, 0, 0), ("take", 1, 1, 1), ("select", 1, 1, 0), ("own", 1, 1, 0), ("near", 1, 0, 1), ("weigh", 1, 0),
-    ("near", 1, 0, 2), ("near", 1, 0, 3), ("take", 1, 1, 2), ("expert", 1, 0, 0), ("take", 1, 1, 3), ("select", 1, 1, 1),
-    ("own", 1, 1, 1), ("near", 1, 1, 0), ("near", 1, 1, 1), ("expert", 1, 0, 1), ("near", 1, 1, 2), ("turn", 1, 0, 2),
-    ("near", 1, 1, 3), ("turn", 1, 0, 3), ("own", 1, 1, 2), ("finish", 1, 0, 0), ("own", 1, 1, 3), ("expert", 1, 1, 1),
-    ("finish", 1, 0, 1), ("expert", 1, 1, 0), ("turn", 1, 1, 2), ("combine", 1, 0, 0), ("turn", 1, 1, 3), ("finish", 1, 1, 0),
-    ("combine", 1, 0, 1), ("combine", 1, 0, 2), ("finish", 1, 1, 1), ("weigh", 1, 1), ("combine", 1, 0, 3),
-    ("combine", 1, 1, 0), ("combine", 1, 1, 1), ("combine", 1, 1, 2), ("combine", 1, 1, 3),
+    ("select", 0, 1, 0), ("own", 0, 1, 0), ("select", 0, 0, 1), ("select", 0, 0, 0), ("own", 0, 0, 0), ("near", 0, 0, 0),
+    ("weigh", 0, 0), ("own", 0, 0, 1), ("near", 0, 0, 1), ("near", 0, 0, 2), ("select", 0, 1, 1), ("own", 0, 0, 2),
+    ("near", 0, 1, 0), ("expert", 0, 0, 1), ("near", 0, 1, 1), ("own", 0, 1, 1), ("near", 0, 1, 2), ("expert", 0, 0, 0),
+    ("turn", 0, 0, 2), ("own", 0, 1, 2), ("finish", 0, 0, 0), ("weigh", 0, 1), ("expert", 0, 1, 1), ("finish", 0, 0, 1),
+    ("expert", 0, 1, 0), ("combine", 0, 0, 0), ("finish", 0, 1, 0), ("combine", 0, 0, 1), ("turn", 0, 1, 2),
+    ("combine", 0, 0, 2), ("finish", 0, 1, 1), ("take", 1, 0, 0), ("select", 1, 0, 0), ("combine", 0, 1, 0), ("own", 1, 0, 0),
+    ("combine", 0, 1, 1), ("take", 1, 0, 1), ("own", 1, 0, 1), ("combine", 0, 1, 2), ("take", 1, 0, 2), ("select", 1, 0, 1),
+    ("own", 1, 0, 2), ("near", 1, 0, 0), ("take", 1, 1, 0), ("select", 1, 1, 0), ("select", 1, 1, 1), ("take", 1, 1, 1),
+    ("near", 1, 0, 1), ("near", 1, 0, 2), ("weigh", 1, 0), ("own", 1, 1, 0), ("take", 1, 1, 2), ("near", 1, 1, 0),
+    ("expert", 1, 0, 1), ("near", 1, 1, 1), ("near", 1, 1, 2), ("own", 1, 1, 1), ("expert", 1, 0, 0), ("own", 1, 1, 2),
+    ("weigh", 1, 1), ("expert", 1, 1, 1), ("finish", 1, 0, 0), ("turn", 1, 0, 2), ("expert", 1, 1, 0), ("finish", 1, 1, 0),
+    ("finish", 1, 0, 1), ("combine", 1, 0, 0), ("finish", 1, 1, 1), ("turn", 1, 1, 2), ("combine", 1, 1, 0),
+    ("combine", 1, 0, 1), ("combine", 1, 0, 2), ("combine", 1, 1, 1), ("combine", 1, 1, 2),
 )
 
 

time: 192 us -> 188 us (0.979)
  Pallas kernels: 186 us -> 182 us
    pallas_call x1, Pallas kernels: 186 us -> 182 us  [body(): pl.pallas_call(functools.partial(relay, pipe_count), out_shape=(result, r...]
where the time goes in v4:
time: 188 us; the launch traced here: 187 us
  Pallas kernels  182 us (97%)
  local copies, waits for them, and re-layouts  4.21 us (2%)
    pallas_call x1, Pallas kernels, body(): pl.pallas_call(functools.partial(relay, pipe_count), out_shape=(result, r...  182 us
    unnamed x4, local copies, waits for them, and re-layouts  4.21 us

profile of v4, /device:TPU:100, one launch (start us, length us, event | category | flops | bytes accessed | tf_op | source)
XLA Modules:
  0.0 186.6 jit_solution(3702335718793543335)
XLA Ops:
  0.6 181.8 %shard_map.104 = (bf16[2,1,128,3584]{3,2,1,0:T(8,128)(2,1)}, bf16[2,1,128,3584]{3,2,1,0:T(8,128)(2,1)}) custom-call(bf16[1,128,3584]{2,1,0:T(8,128)(2,1)} %a_in.1, bf16[1,128,3584]{2,1,0:T(8,128)(2,1)} %b_in.1, bf16[1,128,3584]{2,1,0:T(8,128)(2,1)} %later_in.1, s32[4,128]{1,0:T(4,128)} %bitcast.7, bf16[2,3584]{1,0:T(2,128)(2,1)} %bitcast.6, ...), custom_call_target="tpu_custom_call" | custom-call | flops 14092861440 | bytes 44040192 | tf_op jit(solution)/shard_map/pallas_call | solution.py:389
  182.4 0.0 copy-start
  182.4 3.0 %copy.13 = bf16[2,1,128,3584]{3,2,1,0:T(8,128)(2,1)} copy(bf16[2,1,128,3584]{3,2,1,0:T(8,128)(2,1)} %get-tuple-element.4) | data formatting | bytes 3670016
  185.4 0.0 copy-done
  185.4 1.2 copy.14
Async XLA Ops:
  182.4 3.0 %copy-start = (bf16[2,1,128,3584]{3,2,1,0:T(8,128)(2,1)S(1)}, bf16[2,1,128,3584]{3,2,1,0:T(8,128)(2,1)}, u32[]{:S(2)}) copy-start(bf16[2,1,128,3584]{3,2,1,0:T(8,128)(2,1)} %get-tuple-element.5) | copy-start | bytes 5505028

commit v5 on v4

--- a/solution.py
+++ b/solution.py
@@ -386,7 +386,7 @@
         outside = pl.BlockSpec(memory_space=pl.ANY)
         result = jax.ShapeDtypeStruct((steps, 1, tokens, width), BF16)
         dma = pltpu.SemaphoreType.DMA
-        return pl.pallas_call(
+        made = pl.pallas_call(
             functools.partial(relay, pipe_count),
             out_shape=(result, result),
             in_specs=[outside] * 3 + [whole] * 3 + [outside] * 3,
@@ -443,6 +443,30 @@
             ),
         )(a_init, b_init, incoming, chosen, gain[0], jnp.swapaxes(router[0], 1, 2), w_gate, w_up, w_down)
 
+        def hand_over(a_from, b_from, a_to, b_to, held, sems):
+            rows = tokens // 4
+            parts = [(n, m, pl.ds(q * rows, rows), sems.at[n, m, q]) for n in range(steps) for m in (0, 1) for q in range(4)]
+            into = [
+                pltpu.make_async_copy((a_from, b_from)[m].at[n, 0, at], held.at[n, m, at], sem) for n, m, at, sem in parts
+            ]
+            out = [pltpu.make_async_copy(held.at[n, m, at], (a_to, b_to)[m].at[n, 0, at], sem) for n, m, at, sem in parts]
+            for copy in into:
+                copy.start()
+            for first, second in zip(into, out):
+                first.wait()
+                second.start()
+            for copy in out:
+                copy.wait()
+
+        return pl.pallas_call(
+            hand_over,
+            out_shape=(result, result),
+            in_specs=[outside] * 2,
+            out_specs=(outside, outside),
+            scratch_shapes=[pltpu.VMEM((steps, 2, tokens, width), BF16), dma((steps, 2, 4))],
+        )(*made)
+
+
     placed = (
         P("pipe", "expert", None),
         P("pipe", "expert", None),

time: 188 us -> 188 us (level)
  local copies, waits for them, and re-layouts: 4.21 us -> 0 us
  Pallas kernels: 182 us -> 185 us
    unnamed x4 -> x0, local copies, waits for them, and re-layouts: 4.21 us -> none
    pallas_call x0 -> x1, Pallas kernels: none -> 3.63 us  [body(): pl.pallas_call(hand_over, out_shape=(result, result), in_specs=[outside]...]
where the time goes in v5:
time: 188 us; the launch traced here: 186 us
  Pallas kernels  185 us (98%)
    pallas_call x1, Pallas kernels, body(): pl.pallas_call(functools.partial(relay, pipe_count), out_shape=(result, r...  182 us

profile of v5, /device:TPU:100, one launch (start us, length us, event | category | flops | bytes accessed | tf_op | source)
XLA Modules:
  0.0 186.2 jit_solution(4091492441099600994)
XLA Ops:
  0.6 181.8 %shard_map.104 = (bf16[2,1,128,3584]{3,2,1,0:T(8,128)(2,1)}, bf16[2,1,128,3584]{3,2,1,0:T(8,128)(2,1)}) custom-call(bf16[1,128,3584]{2,1,0:T(8,128)(2,1)} %a_in.1, bf16[1,128,3584]{2,1,0:T(8,128)(2,1)} %b_in.1, bf16[1,128,3584]{2,1,0:T(8,128)(2,1)} %later_in.1, s32[4,128]{1,0:T(4,128)} %bitcast.7, bf16[2,3584]{1,0:T(2,128)(2,1)} %bitcast.6, ...), custom_call_target="tpu_custom_call" | custom-call | flops 14092861440 | bytes 44040192 | tf_op jit(solution)/shard_map/pallas_call | solution.py:389
  182.4 3.6 %shard_map.105 = (bf16[2,1,128,3584]{3,2,1,0:T(8,128)(2,1)}, bf16[2,1,128,3584]{3,2,1,0:T(8,128)(2,1)}) custom-call(bf16[2,1,128,3584]{3,2,1,0:T(8,128)(2,1)} %get-tuple-element.4.a_from, bf16[2,1,128,3584]{3,2,1,0:T(8,128)(2,1)} %get-tuple-element.5.b_from), custom_call_target="tpu_custom_call" | custom-call | tf_op jit(solution)/shard_map/pallas_call | solution.py:461
